TPU v7x, 256 devices: a whole 4x4x8 slice. The times are simulated.
256 devices in a mesh: ctx: 16 (over x_lo, z), head: 16 (over x_hi, y, core).
Axes of the slice: x: 4 (x_hi: 2, x_lo: 2; x = x_hi * 2 + x_lo), y: 4, z: 8, core: 2. Of those that a mesh axis runs over, the one named last changes fastest.
Arguments:
- queries: bfloat16 [4096, 64, 192], P('ctx', 'head'), may hold values from -6 to 6
- latent_cache: bfloat16 [4096, 576], P('ctx'), may hold values from -260 to 260
- key_absorb: bfloat16 [64, 128, 512], P('head'), may hold values from -0.5 to 0.5
- value_absorb: bfloat16 [64, 512, 128], P('head'), may hold values from -0.75 to 0.75
- out_weight: bfloat16 [8192, 7168], P('head'), may hold values from -0.75 to 0.75
- span_order: int32 [32], replicated, may hold values from 0 to 31, as said below
Outputs:
- mixed: bfloat16 [4096, 7168], P('ctx', 'head')
Inputs may be any that keep to these rules, and one draw needn't show every extreme that they name: `span_order`: entries 2 d and 2 d + 1 are the spans of device d along ctx; every span number appears once, and the two spans of a device sum to 31.
All inputs are finite; a program needn't handle non-finite values.
Results may differ from a plain program's by a relative error of at most 0.024.
Values may be sent and summed in bfloat16 or wider, within the bound.
No kernel may reach another device: no remote copies, remote signals or barrier semaphores. Data moves between devices by JAX's collectives and lax.ppermute only.
A program may use at most 64 MiB of HBM per device.

v0:
```python
import math

import jax
import jax.numpy as jnp
from jax import lax
from jax.sharding import PartitionSpec as P

NEG_FILL = -1e30


def rotate(values, angle_pos):
    half_width = values.shape[-1] // 2
    inverse = 10000.0 ** (-jnp.arange(half_width, dtype=jnp.float32) * 2.0 / values.shape[-1])
    angles = angle_pos.astype(jnp.float32)[..., None] * inverse
    front_half = values[..., :half_width]
    back_half = values[..., half_width:]
    cosine = jnp.cos(angles)
    sine_part = jnp.sin(angles)
    return jnp.concatenate(
        [front_half * cosine - back_half * sine_part, front_half * sine_part + back_half * cosine],
        axis=-1,
    )


def span_lookup(span_order, slots):
    slot_table = jnp.arange(span_order.shape[0], dtype=jnp.int32)
    hits = slots[:, None] == slot_table[None, :]
    return jnp.sum(jnp.where(hits, span_order[None, :], 0), axis=1)


def token_positions(span_order, first_row, count, span_len):
    row_index = first_row + jnp.arange(count, dtype=jnp.int32)
    return span_lookup(span_order, row_index // span_len) * span_len + row_index % span_len


def body(queries, latent_cache, key_absorb, value_absorb, out_weight, span_order):
    tok_rows, head_count, query_width = queries.shape
    nope_width = key_absorb.shape[1]
    latent_width = key_absorb.shape[2]
    span_len = tok_rows // 2
    score_scale = 1.0 / math.sqrt(query_width)
    own_start = lax.axis_index("ctx") * tok_rows
    own_positions = token_positions(span_order, own_start, tok_rows, span_len)
    rotated = rotate(latent_cache[:, latent_width:].astype(jnp.float32), own_positions).astype(
        jnp.bfloat16
    )
    keyed = jnp.concatenate([latent_cache[:, :latent_width], rotated], axis=1)
    query_latent = jnp.einsum(
        "thn,hnl->thl", queries[:, :, :nope_width], key_absorb, preferred_element_type=jnp.float32
    ).astype(jnp.bfloat16)
    query_rope = rotate(
        queries[:, :, nope_width:].astype(jnp.float32), own_positions[:, None]
    ).astype(jnp.bfloat16)
    absorbed = jnp.concatenate([query_latent, query_rope], axis=2)

    def make_update(query_rows, query_pos, key_block, key_pos):
        latent_part = key_block[:, :latent_width]

        def update(states):
            running_max, running_sum, running_acc = states
            scores = (
                jnp.einsum("thc,kc->thk", query_rows, key_block, preferred_element_type=jnp.float32)
                * score_scale
            )
            visible = key_pos[None, None, :] <= query_pos[:, None, None]
            scores = jnp.where(visible, scores, NEG_FILL)
            new_max = jnp.maximum(running_max, jnp.max(scores, axis=2))
            weights = jnp.where(visible, jnp.exp(scores - new_max[:, :, None]), 0.0)
            new_sum = jnp.sum(weights, axis=2)
            product = jnp.einsum(
                "thk,kl->thl",
                weights.astype(jnp.bfloat16),
                latent_part,
                preferred_element_type=jnp.float32,
            )
            return (new_max, new_sum, product)

        return update

    start_max = jnp.full((span_len, head_count), NEG_FILL, jnp.float32)
    start_sum = jnp.zeros((span_len, head_count), jnp.float32)
    start_acc = jnp.zeros((span_len, head_count, latent_width), jnp.float32)
    initial = ((start_max, start_sum, start_acc), (start_max, start_sum, start_acc))
    span_piece = lax.all_gather(keyed, "ctx", axis=0, tiled=True)
    piece_rows = span_piece.shape[0]
    key_pos = token_positions(span_order, jnp.int32(0), piece_rows, span_len)
    results = []
    for query_half in range(2):
        query_rows = absorbed[query_half * span_len : (query_half + 1) * span_len]
        query_pos = own_positions[query_half * span_len : (query_half + 1) * span_len]
        update = make_update(query_rows, query_pos, span_piece, key_pos)
        results.append(update(initial[query_half]))
    folded = (results[0], results[1])
    context = jnp.concatenate(
        [folded[0][2] / folded[0][1][:, :, None], folded[1][2] / folded[1][1][:, :, None]], axis=0
    ).astype(jnp.bfloat16)
    head_values = jnp.einsum(
        "thl,hlv->thv", context, value_absorb, preferred_element_type=jnp.float32
    ).astype(jnp.bfloat16)
    flat_heads = head_values.reshape(tok_rows, head_count * head_values.shape[2])
    partial_value = jnp.dot(flat_heads, out_weight, preferred_element_type=jnp.float32)
    return lax.psum_scatter(
        partial_value.astype(jnp.bfloat16), "head", scatter_dimension=1, tiled=True
    )


def solution(mesh):
    return jax.shard_map(
        body,
        mesh=mesh,
        in_specs=(
            P("ctx", "head", None),
            P("ctx", None),
            P("head", None, None),
            P("head", None, None),
            P("head", None),
            P(),
        ),
        out_specs=P("ctx", "head"),
        check_vma=False,
    )
```

profile of v0, /device:TPU:1, one launch (start us, length us, event | category | flops | bytes accessed | tf_op | source)
XLA Modules:
  0.0 228.9 jit_solution(4526738805928733324)
XLA Ops:
  6.6 0.8 slice_convert_fusion.1
  7.4 1.0 slice.46
  8.4 0.7 select_reduce_fusion.1
  9.1 0.2 multiply_cosine_fusion
  9.3 0.7 pad_maximum_fusion.1
  10.1 0.0 all-gather.2.cloned.1.call-update
  10.1 0.0 reduce-scatter.2.cloned.1.call-start
  10.2 0.8 select_reduce_fusion
  11.0 0.9 slice_convert_fusion
  12.0 1.4 fusion.24
  13.4 0.1 pad_maximum_fusion
  13.5 0.6 broadcast_compare_fusion.1
  14.2 84.1 %all-gather.2.cloned.1.call-done = bf16[4096,576]{0,1:T(8,128)(2,1)} async-done(((bf16[256,576]{0,1:T(8,128)(2,1)}), bf16[4096,576]{0,1:T(8,128)(2,1)}) %all-gather.2.cloned.1.call-update) | async-done | bytes 4718608 | tf_op jit(solution)/shard_map/all_gather | solution.py:84
  98.2 6.3 %fusion.1 = (f32[128,4]{0,1:T(4,128)S(1)}, f32[128,4,4096]{2,0,1:T(8,128)S(1)}) fusion(pred[128,4096]{1,0:T(8,128)(4,1)S(1)} %get-tuple-element.12, bf16[4096,576]{0,1:T(8,128)(2,1)} %all-gather.2.cloned.1.call-done, bf16[256,4,576]{0,2,1:T(8,128)(2,1)S(1)} %pad_maximum_fusion), kind=kOutput, calls=%fused_computation.6 | convolution fusion | flops 2422210048 | bytes 14223360 | tf_op jit(solution)/shard_map/thc,kc->thk/dot_general | solution.py:62
  104.6 4.4 %fusion = (f32[128,4]{0,1:T(4,128)S(1)}, f32[128,4,4096]{2,0,1:T(8,128)S(1)}) fusion(pred[128,4096]{1,0:T(8,128)(4,1)S(1)} %get-tuple-element.11, bf16[4096,576]{0,1:T(8,128)(2,1)S(1)} %copy-done.1, bf16[256,4,576]{0,2,1:T(8,128)(2,1)S(1)} %pad_maximum_fusion), kind=kOutput, calls=%fused_computation.5 | convolution fusion | flops 2422210048 | bytes 14223360 | tf_op jit(solution)/shard_map/thc,kc->thk/dot_general | solution.py:62
  109.0 4.9 %fusion.2 = (f32[128,4]{0,1:T(4,128)S(1)}, f32[128,4]{0,1:T(4,128)S(1)}) fusion(f32[128,4,4096]{2,0,1:T(8,128)S(1)} %get-tuple-element.22, f32[128,4]{0,1:T(4,128)S(1)} %broadcast_maximum_fusion.1, pred[128,4096]{1,0:T(8,128)(4,1)S(1)} %get-tuple-element.11, f32[128,4]{0,1:T(4,128)S(1)} %broadcast_maximum_fusion, f32[128,4,4096]{2,0,1:T(8,128)S(1)} %get-tuple-element.20, ...), kind=kLoop, calls=%fused_computation.7 | loop fusion | flops 20970496 | bytes 17833984 | tf_op jit(solution)/shard_map/reduce_sum | solution.py:69
  114.0 0.0 slice-start
  114.0 4.9 %divide_convert_fusion = bf16[128,4,512]{2,0,1:T(8,128)(2,1)S(1)} fusion(bf16[4096,576]{0,1:T(8,128)(2,1)} %all-gather.2.cloned.1.call-done, f32[128,4,4096]{2,0,1:T(8,128)S(1)} %get-tuple-element.20, f32[128,4]{0,1:T(4,128)S(1)} %broadcast_maximum_fusion, pred[128,4096]{1,0:T(8,128)(4,1)S(1)} %get-tuple-element.12, f32[128,4]{0,1:T(4,128)S(1)} %get-tuple-element.24), kind=kOutput, calls=%fused_computation.35 | convolution fusion | flops 2158493696 | bytes 13635584 | tf_op jit(solution)/shard_map/thk,kl->thl/dot_general | solution.py:70
  118.9 0.0 slice-start.1
  118.9 4.9 %divide_convert_fusion.1 = bf16[128,4,512]{2,0,1:T(8,128)(2,1)S(1)} fusion(bf16[4096,576]{0,1:T(8,128)(2,1)} %all-gather.2.cloned.1.call-done, f32[128,4,4096]{2,0,1:T(8,128)S(1)} %get-tuple-element.22, f32[128,4]{0,1:T(4,128)S(1)} %broadcast_maximum_fusion.1, pred[128,4096]{1,0:T(8,128)(4,1)S(1)} %get-tuple-element.11, f32[128,4]{0,1:T(4,128)S(1)} %get-tuple-element.23), kind=kOutput, calls=%fused_computation.36 | convolution fusion | flops 2158493696 | bytes 13635584 | tf_op jit(solution)/shard_map/thk,kl->thl/dot_general | solution.py:70
  123.7 0.5 convolution_convert_fusion.2
  124.3 4.8 %convolution_convert_fusion = bf16[256,7168]{0,1:T(8,128)(2,1)} fusion(bf16[256,512]{0,1:T(8,128)(2,1)S(1)} %bitcast.28, bf16[512,7168]{1,0:T(8,128)(2,1)S(1)} %bitcast.27), kind=kOutput, calls=%fused_computation | convolution fusion | flops 1880883200 | bytes 11272192 | tf_op jit(solution)/shard_map/dot_general | solution.py:101
  129.0 0.0 reduce-scatter.2.cloned.1.call-update
  129.0 93.1 %reduce-scatter.2.cloned.1.call-done = bf16[256,448]{0,1:T(8,128)(2,1)} async-done(((bf16[256,7168]{0,1:T(8,128)(2,1)}), bf16[256,448]{0,1:T(8,128)(2,1)}) %reduce-scatter.2.cloned.1.call-update) | async-done | bytes 229392 | tf_op jit(solution)/shard_map/reduce_scatter | solution.py:102
  (19 shorter events, 0.1 us)
Async XLA Ops:
  6.5 5.4 %copy-start = (bf16[4,128,512]{2,1,0:T(8,128)(2,1)S(1)}, bf16[4,128,512]{2,1,0:T(8,128)(2,1)}, u32[]{:S(2)}) copy-start(bf16[4,128,512]{2,1,0:T(8,128)(2,1)} %param.8) | copy-start | bytes 1572868
  6.5 91.7 %all-gather.2.cloned.1.call-start = ((), (), s32[]{:S(2)}) async-start(), calls=%async_computation.1 | async-start | bytes 5013504 | tf_op jit(solution)/shard_map/all_gather | solution.py:84
  10.1 212.0 %reduce-scatter.2.cloned.1.call-start = ((), (), s32[]{:S(2)}) async-start(), calls=%async_computation.2 | async-start | bytes 3899392 | tf_op jit(solution)/shard_map/reduce_scatter | solution.py:102
  98.2 6.3 %copy-start.1 = (bf16[4096,576]{0,1:T(8,128)(2,1)S(1)}, bf16[4096,576]{0,1:T(8,128)(2,1)}, u32[]{:S(2)}) copy-start(bf16[4096,576]{0,1:T(8,128)(2,1)} %all-gather.2.cloned.1.call-done) | copy-start | bytes 14155780
  114.0 10.3 %slice-start = ((s8[7340032]{0:T(1024)(128)(4,1)}), s8[3145728]{0:T(1024)(128)(4,1)S(1)}, s32[]{:S(2)}) async-start(s8[7340032]{0:T(1024)(128)(4,1)} %bitcast.26), calls=%async_computation.3 | async-start | bytes 6291456
  118.8 4.9 %copy-start.2 = (bf16[4,512,128]{2,1,0:T(8,128)(2,1)S(1)}, bf16[4,512,128]{2,1,0:T(8,128)(2,1)}, u32[]{:S(2)}) copy-start(bf16[4,512,128]{2,1,0:T(8,128)(2,1)} %param.9) | copy-start | bytes 1572868
  118.9 5.4 %slice-start.1 = ((s8[7340032]{0:T(1024)(128)(4,1)}), s8[4194304]{0:T(1024)(128)(4,1)S(1)}, s32[]{:S(2)}) async-start(s8[7340032]{0:T(1024)(128)(4,1)} %bitcast.26), calls=%async_computation.4 | async-start | bytes 8388608
Sparse Core Ops, SparseCore 0:
  10.2 87.9 all-gather.1
  129.2 92.8 reduce-scatter.1
where the time goes:
time: 229 us
  waiting for transfers between devices  177 us (77%)
  matrix products  27.1 us (12%)
  between operations  13.6 us (6%)
  other arithmetic  10 us (4%)
    reduce_scatter x1, waiting for transfers between devices, body(): lax.psum_scatter(partial_value.astype(jnp.bfloat16), 'head', scatter_dime...  93.1 us
    all_gather x1, waiting for transfers between devices, body(): span_piece = lax.all_gather(keyed, 'ctx', axis=0, tiled=True)  84.1 us
    dot_general x2, matrix products, update(): jnp.einsum('thc,kc->thk', query_rows, key_block, preferred_element_type=j...  10.7 us
    dot_general x2, matrix products, update(): jnp.einsum('thk,kl->thl', weights.astype(jnp.bfloat16), latent_part, pref...  9.72 us
    reduce_sum x1, other arithmetic, update(): new_sum = jnp.sum(weights, axis=2)  4.95 us
    dot_general x1, matrix products, body(): jnp.dot(flat_heads, out_weight, preferred_element_type=jnp.float32)  4.76 us
  transfers between devices with their start and end apart: 2, of which 2 were waited for; matrix products, arithmetic and copies ran while one was open for 2% of the time, Pallas kernels for 0%

commit v1 on v0

v1 whole, which is shorter than its diff:
```python
import functools
import math

import jax
import jax.numpy as jnp
import numpy as np
from jax import lax
from jax.experimental import pallas as pl
from jax.experimental.pallas import tpu as pltpu
from jax.sharding import PartitionSpec as P

BF16 = jnp.bfloat16
F32 = jnp.float32
AXES = ("ctx", "head")
NXL, NZ, NXH, NY, NC = 2, 8, 2, 4, 2
SPAN = 128
LAT = 512
ROPE = 64
PIECE = 144
HEADS = 4
NEG = -1e30
VMEM = pltpu.CompilerParams(vmem_limit_bytes=56 * 1024 * 1024)


def device(x, y, z, c):
    x, y, z = x % 4, y % NY, z % NZ
    return ((((x % 2) * NZ + z) * NXH + x // 2) * NY + y) * NC + c


def routes(step):
    pairs = []
    for x in range(4):
        for y in range(NY):
            for z in range(NZ):
                for c in range(NC):
                    pairs.append((device(x, y, z, c), device(*step(x, y, z, c))))
    return pairs


def way(c):
    return 1 - 2 * c


def send(value, step):
    return lax.ppermute(value, AXES, routes(step))


def along(dx=0, dy=0, dz=0):
    return lambda x, y, z, c: (x + dx * way(c), y + dy * way(c), z + dz * way(c), c)


def swap(x, y, z, c):
    return x, y, z, 1 - c


def tables():
    inverse = 10000.0 ** (-np.arange(ROPE // 2, dtype=np.float64) * 2.0 / ROPE)
    inverse = np.concatenate([inverse, inverse])[None, :]
    sign = np.concatenate([-np.ones(ROPE // 2), np.ones(ROPE // 2)])[None, :]
    rows = np.arange(SPAN, dtype=np.float64)[:, None] * inverse
    spans = np.arange(32, dtype=np.float64)[:, None] * SPAN * inverse
    table = np.concatenate(
        [
            np.concatenate([np.cos(rows), sign * np.sin(rows)], axis=1),
            np.concatenate([np.cos(spans), sign * np.sin(spans)], axis=1),
        ],
        axis=0,
    ).astype(np.float32)
    swapper = np.roll(np.eye(ROPE, dtype=np.float32), ROPE // 2, axis=1)
    return jnp.asarray(table), jnp.asarray(swapper, dtype=BF16)


def cos_sin(table_ref, span):
    cr, sr = table_ref[0:SPAN, 0:ROPE], table_ref[0:SPAN, ROPE : 2 * ROPE]
    row = table_ref[pl.ds(SPAN + span, 1), :]
    cs, ss = row[:, 0:ROPE], row[:, ROPE : 2 * ROPE]
    return cr * cs - sr * ss, cr * ss + sr * cs


def rotated(values, cos, sin, swapper):
    other = jnp.dot(values, swapper, preferred_element_type=F32)
    return values.astype(F32) * cos + other * sin


def me():
    ctx, head = lax.axis_index("ctx"), lax.axis_index("head")
    return ctx // NZ, ctx % NZ, head // (NY * NC), (head // NC) % NY, head % NC


def span_of(order_ref, xl, z, half):
    ctx = xl * NZ + lax.rem(z + 2 * NZ, NZ)
    a, b = order_ref[2 * ctx], order_ref[2 * ctx + 1]
    return jnp.where(half == 0, jnp.minimum(a, b), jnp.maximum(a, b))


def own_rows(order_ref, half):
    ctx = lax.axis_index("ctx")
    swapped = (order_ref[2 * ctx] > order_ref[2 * ctx + 1]).astype(jnp.int32)
    return pl.multiple_of(SPAN * (swapped ^ half), SPAN)


SMEM_SPEC = pl.BlockSpec(memory_space=pltpu.SMEM)
VMEM_SPEC = pl.BlockSpec(memory_space=pltpu.VMEM)
ANY_SPEC = pl.BlockSpec(memory_space=pl.ANY)


def pack_kernel(order_ref, cache_ref, table_ref, swapper_ref, own_ref, slice_ref, first_ref):
    xl, z, xh, y, c = me()
    for half in range(2):
        rows = own_rows(order_ref, half)
        span = span_of(order_ref, xl, z, half)
        latent = cache_ref[pl.ds(rows, SPAN), 0:LAT]
        raw = cache_ref[pl.ds(rows, SPAN), LAT : LAT + ROPE]
        cos, sin = cos_sin(table_ref, span)
        turned = rotated(raw, cos, sin, swapper_ref[...])
        tiles = [
            jnp.concatenate(
                [turned[32 * j : 32 * j + 16], turned[32 * j + 16 : 32 * j + 32]], axis=1
            )
            for j in range(4)
        ]
        packed = jnp.concatenate(tiles, axis=1).astype(BF16)
        own_ref[half, 0:SPAN, :] = latent
        own_ref[half, SPAN:PIECE, :] = packed

        @pl.when(y % 2 == half)
        def _():
            slice_ref[0:SPAN, :] = latent
            slice_ref[SPAN:PIECE, :] = packed

        @pl.when(c == half)
        def _():
            first_ref[0:SPAN, :] = latent
            first_ref[SPAN:PIECE, :] = packed


def pack(order, cache, table, swapper):
    return pl.pallas_call(
        pack_kernel,
        out_shape=(
            jax.ShapeDtypeStruct((2, PIECE, LAT), BF16),
            jax.ShapeDtypeStruct((PIECE, LAT), BF16),
            jax.ShapeDtypeStruct((PIECE, LAT), BF16),
        ),
        in_specs=[SMEM_SPEC, VMEM_SPEC, VMEM_SPEC, VMEM_SPEC],
        out_specs=(VMEM_SPEC,) * 3,
        compiler_params=VMEM,
        name="pack_keys",
    )(order, cache, table, swapper)


def absorb_kernel(order_ref, query_ref, absorb_ref, table_ref, swapper_ref, out_ref):
    xl, z, xh, y, c = me()
    for half in range(2):
        rows = own_rows(order_ref, half)
        cos, sin = cos_sin(table_ref, span_of(order_ref, xl, z, half))
        for h in range(HEADS):
            q = query_ref[h, pl.ds(rows, SPAN), :]
            nope, raw = q[:, 0:128], q[:, 128:192]
            part = jnp.dot(nope, absorb_ref[h], preferred_element_type=F32).astype(BF16)
            turned = rotated(raw, cos, sin, swapper_ref[...])
            tail = jnp.concatenate([turned, jnp.zeros_like(turned)], axis=1).astype(BF16)
            out_ref[half, h * SPAN : (h + 1) * SPAN, 0:LAT] = part
            out_ref[half, h * SPAN : (h + 1) * SPAN, LAT : LAT + 128] = tail


def absorb(order, queries, key_absorb, table, swapper):
    return pl.pallas_call(
        absorb_kernel,
        out_shape=jax.ShapeDtypeStruct((2, HEADS * SPAN, LAT + 128), BF16),
        in_specs=[SMEM_SPEC] + [VMEM_SPEC] * 4,
        out_specs=VMEM_SPEC,
        compiler_params=VMEM,
        name="absorb_queries",
    )(order, queries, key_absorb, table, swapper)


def attend_kernel(
    order_ref, q_ref, va_ref, own, first, b12, y12, x12, d12, b3, y3, x3, d3, b4, y4, x4, d4, g1, g2,
    out_ref, keys, krope, scores, peak, total, acc, sems,
):
    xl, z, xh, y, c = me()
    s = y % 2
    w = 1 - 2 * c
    copies = []

    def fetch(src, dst):
        copy = pltpu.make_async_copy(src, dst, sems.at[len(copies)])
        copy.start()
        copies.append(copy)

    for half in range(2):
        fetch(own.at[half], keys.at[span_of(order_ref, xl, z, half)])
    fetch(first, keys.at[span_of(order_ref, 1 - xl, z, c)])
    fetch(g1.at[pl.ds(0, PIECE)], keys.at[span_of(order_ref, 1 - xl, z, 1 - c)])
    kinds = ((xl, s), (xl, 1 - s), (1 - xl, s), (1 - xl, 1 - s))
    for k, (bundle, third, fourth) in enumerate(((b12, b3, b4), (y12, y3, y4), (x12, x3, x4), (d12, d3, d4))):
        px, ph = kinds[k]
        for t in (1, 2):
            here = span_of(order_ref, px, z - w * t, ph)
            there = span_of(order_ref, px, z + w * t, ph)
            fetch(bundle.at[pl.ds((t - 1) * PIECE, PIECE)], keys.at[here])
            fetch(g1.at[pl.ds((1 + 2 * k + t - 1) * PIECE, PIECE)], keys.at[there])
        fetch(third, keys.at[span_of(order_ref, px, z - 3 * w, ph)])
        fetch(g2.at[pl.ds(k * PIECE, PIECE)], keys.at[span_of(order_ref, px, z + 3 * w, ph)])
        far = span_of(order_ref, px, z + 4, ph)
        mine = pl.multiple_of(256 * c, 256)
        other = pl.multiple_of(256 * (1 - c), 256)
        fetch(fourth, keys.at[far, :, pl.ds(mine, 256)])
        fetch(
            g2.at[pl.ds((4 + k // 2) * PIECE, PIECE), pl.ds(256 * (k % 2), 256)],
            keys.at[far, :, pl.ds(other, 256)],
        )
    for copy in copies:
        copy.wait()

    def unpack(i, _):
        packed = keys[i, SPAN:PIECE, :].astype(F32)
        zero = jnp.zeros((16, ROPE), F32)
        for j in range(8):
            part = jnp.concatenate([packed[:, ROPE * j : ROPE * (j + 1)], zero], axis=1)
            krope[pl.ds(pl.multiple_of(i * SPAN + 16 * j, 16), 16), :] = part.astype(BF16)
        return 0

    lax.fori_loop(0, 32, unpack, 0, unroll=4)

    lower = span_of(order_ref, xl, z, 0)
    upper = 31 - lower
    count = lower // 2
    scale = math.log2(math.e) / math.sqrt(192.0)
    wide = (((1,), (1,)), ((), ()))

    def score(half, block):
        latent = keys[pl.ds(2 * block, 2), 0:SPAN, :].reshape(2 * SPAN, LAT)
        turned = krope[pl.ds(pl.multiple_of(block * 2 * SPAN, 2 * SPAN), 2 * SPAN), :]
        q = q_ref[half]
        return lax.dot_general(q[:, 0:LAT], latent, wide, preferred_element_type=F32) + lax.dot_general(
            q[:, LAT:], turned, wide, preferred_element_type=F32
        )

    for half, span in ((0, lower), (1, upper)):
        block = span // 2
        value = score(half, block)
        row = lax.rem(lax.broadcasted_iota(jnp.int32, value.shape, 0), SPAN) + (span % 2) * SPAN
        column = lax.broadcasted_iota(jnp.int32, value.shape, 1)
        value = jnp.where(column <= row, value, NEG)
        scores[15 + half] = value
        peak[half] = jnp.maximum(value[:, 0:128], value[:, 128:256])

    def place(i):
        half = (i >= count).astype(jnp.int32)
        return half, i - half * count

    def first_pass(i, _):
        half, block = place(i)
        value = score(half, block)
        scores[i] = value
        peak[half] = jnp.maximum(peak[half], jnp.maximum(value[:, 0:128], value[:, 128:256]))
        return 0

    lax.fori_loop(0, 15, first_pass, 0)
    for half in range(2):
        top = jnp.max(peak[half], axis=1, keepdims=True) * scale
        peak[half] = jnp.broadcast_to(top, (HEADS * SPAN, 128))

    def weigh(i, half, block):
        top = peak[half]
        value = scores[i]
        left = jnp.exp2(value[:, 0:128] * scale - top)
        right = jnp.exp2(value[:, 128:256] * scale - top)
        weights = jnp.concatenate([left.astype(BF16), right.astype(BF16)], axis=1)
        latent = keys[pl.ds(2 * block, 2), 0:SPAN, :].reshape(2 * SPAN, LAT)
        return left + right, jnp.dot(weights, latent, preferred_element_type=F32)

    for half, span in ((0, lower), (1, upper)):
        some, product = weigh(15 + half, half, span // 2)
        total[half] = some
        acc[half] = product

    def second_pass(i, _):
        half, block = place(i)
        some, product = weigh(i, half, block)
        total[half] += some
        acc[half] += product
        return 0

    lax.fori_loop(0, 15, second_pass, 0)

    for half in range(2):
        rows = own_rows(order_ref, half)
        for h in range(HEADS):
            part = slice(h * SPAN, (h + 1) * SPAN)
            bottom = jnp.sum(total[half, part, :], axis=1, keepdims=True)
            context = (acc[half, part, :] / bottom).astype(BF16)
            value = jnp.dot(context, va_ref[h], preferred_element_type=F32)
            out_ref[pl.ds(rows, SPAN), h * 128 : (h + 1) * 128] = value.astype(BF16)


def attend(order, q, value_absorb, pieces):
    return pl.pallas_call(
        attend_kernel,
        out_shape=jax.ShapeDtypeStruct((2 * SPAN, HEADS * 128), BF16),
        in_specs=[SMEM_SPEC, VMEM_SPEC, VMEM_SPEC] + [ANY_SPEC] * len(pieces),
        out_specs=VMEM_SPEC,
        scratch_shapes=[
            pltpu.VMEM((32, PIECE, LAT), BF16),
            pltpu.VMEM((32 * SPAN, 128), BF16),
            pltpu.VMEM((17, HEADS * SPAN, 2 * SPAN), F32),
            pltpu.VMEM((2, HEADS * SPAN, 128), F32),
            pltpu.VMEM((2, HEADS * SPAN, 128), F32),
            pltpu.VMEM((2, HEADS * SPAN, LAT), F32),
            pltpu.SemaphoreType.DMA((48,)),
        ],
        compiler_params=VMEM,
        cost_estimate=pl.CostEstimate(flops=6_000_000_000, bytes_accessed=8_000_000, transcendentals=2_200_000),
        name="attend",
    )(order, q, value_absorb, *pieces)


def columns_kernel(weight_ref, keep_ref, give_ref):
    c = lax.axis_index("head") % NC
    left = weight_ref[:, 0:448]
    right = weight_ref[:, 448:896]

    @pl.when(c == 0)
    def _():
        keep_ref[0] = left
        give_ref[0] = right

    @pl.when(c == 1)
    def _():
        keep_ref[0] = right
        give_ref[0] = left


def split_columns(weight):
    rows = weight.shape[0]
    return pl.pallas_call(
        columns_kernel,
        grid=(8,),
        out_shape=(jax.ShapeDtypeStruct((8, rows, 448), BF16),) * 2,
        in_specs=[pl.BlockSpec((rows, 896), lambda k: (0, k))],
        out_specs=(pl.BlockSpec((1, rows, 448), lambda k: (k, 0, 0)),) * 2,
        compiler_params=VMEM,
        cost_estimate=pl.CostEstimate(flops=0, bytes_accessed=15_000_000, transcendentals=0),
        name="split_columns",
    )(weight)


OFFSETS = [(1, 2), (1, 1), (1, 3), (0, 2), (1, 0), (0, 1), (0, 3), (0, 0)]


def project_kernel(own_ref, other_ref, keep_ref, got_ref, *rest):
    outs, (keep, got, sems) = rest[:8], rest[8:]
    xl, z, xh, y, c = me()
    copies = []
    for r, (dx, dy) in enumerate(OFFSETS):
        k = lax.rem(xh + dx, NXH) * NY + lax.rem(y + dy, NY)
        pair = (
            pltpu.make_async_copy(keep_ref.at[k], keep.at[r], sems.at[0, r]),
            pltpu.make_async_copy(got_ref.at[k], got.at[r], sems.at[1, r]),
        )
        for copy in pair:
            copy.start()
        copies.append(pair)
    for r in range(8):
        for copy in copies[r]:
            copy.wait()
        outs[r][...] = (
            jnp.dot(own_ref[...], keep[r], preferred_element_type=F32)
            + jnp.dot(other_ref[...], got[r], preferred_element_type=F32)
        ).astype(BF16)


def project(own, other, keep, got):
    rows = own.shape[0]
    return pl.pallas_call(
        project_kernel,
        out_shape=(jax.ShapeDtypeStruct((rows, 448), BF16),) * 8,
        in_specs=[VMEM_SPEC, VMEM_SPEC, ANY_SPEC, ANY_SPEC],
        out_specs=(VMEM_SPEC,) * 8,
        scratch_shapes=[
            pltpu.VMEM((8, 512, 448), BF16),
            pltpu.VMEM((8, 512, 448), BF16),
            pltpu.SemaphoreType.DMA((2, 8)),
        ],
        compiler_params=VMEM,
        cost_estimate=pl.CostEstimate(flops=1_900_000_000, bytes_accessed=8_000_000, transcendentals=0),
        name="project",
    )(own, other, keep, got)


def body(queries, latent_cache, key_absorb, value_absorb, out_weight, span_order):
    table, swapper = tables()
    own, piece, first_half = pack(span_order, latent_cache, table, swapper)

    first = send(first_half, along(dx=1))
    c = lax.axis_index("head") % NC
    columns = jnp.where(c == 0, piece[:, 0:256], piece[:, 256:512])
    b1 = send(piece, along(dz=1))
    b2 = send(piece, along(dz=2))
    b3 = send(piece, along(dz=3))
    b4 = send(columns, along(dz=4))
    b12 = jnp.concatenate([b1, b2], axis=0)
    ways = (along(dy=1), along(dx=1), along(dx=1, dy=1))
    y12, x12, d12 = (send(b12, step) for step in ways)
    y3, x3, d3 = (send(b3, step) for step in ways)
    y4, x4, d4 = (send(b4, step) for step in ways)
    g1 = send(jnp.concatenate([first, b12, y12, x12, d12], axis=0), swap)
    g2 = send(
        jnp.concatenate(
            [b3, y3, x3, d3, jnp.concatenate([b4, y4], axis=1), jnp.concatenate([x4, d4], axis=1)], axis=0
        ),
        swap,
    )

    q = absorb(span_order, queries.transpose(1, 0, 2), key_absorb, table, swapper)
    keep, give = split_columns(out_weight)
    got = send(give, swap)
    pieces = (own, first, b12, y12, x12, d12, b3, y3, x3, d3, b4, y4, x4, d4, g1, g2)
    values = attend(span_order, q, value_absorb, pieces)
    other = send(values, swap)
    terms = project(values, other, keep, got)
    landed = [
        term if (dx, dy) == (0, 0) else send(term, lambda x, y, z, c, dx=dx, dy=dy: (x + 2 * dx, y + dy, z, c))
        for term, (dx, dy) in zip(terms, OFFSETS)
    ]
    return functools.reduce(jnp.add, [term.astype(F32) for term in landed]).astype(BF16)


def solution(mesh):
    return jax.shard_map(
        body,
        mesh=mesh,
        in_specs=(
            P("ctx", "head", None),
            P("ctx", None),
            P("head", None, None),
            P("head", None, None),
            P("head", None),
            P(),
        ),
        out_specs=P("ctx", "head"),
        check_vma=False,
    )
```

time: 229 us -> 141 us (0.62)
  waiting for transfers between devices: 177 us -> 25.6 us
  starting transfers between devices: 0.04 us -> 52.5 us
  Pallas kernels: 0 us -> 39.1 us
  matrix products: 27.1 us -> 0 us
  local copies, waits for them, and re-layouts: 1 us -> 20.5 us
  between operations: 13.6 us -> 0.22 us
  other arithmetic: 10 us -> 2.18 us
    reduce_scatter x1 -> x0, waiting for transfers between devices: 93.1 us -> none  [body(): lax.psum_scatter(partial_value.astype(jnp.bfloat16), 'head', scatter_dime...]
    all_gather x1 -> x0, waiting for transfers between devices: 84.1 us -> none  [body(): span_piece = lax.all_gather(keyed, 'ctx', axis=0, tiled=True)]
    ppermute x0 -> x25, starting transfers between devices: none -> 52.5 us  [send(): return lax.ppermute(value, AXES, routes(step))]
    pallas_call x0 -> x5, Pallas kernels: none -> 39.1 us  [the longest x1 17.6 us: attend(): pl.pallas_call(attend_kernel, out_shape=jax.ShapeDtypeStruct((2 * SPAN, H...]
    dot_general x7 -> x0, matrix products: 27.1 us -> none  [the longest x2 10.7 us: update(): jnp.einsum('thc,kc->thk', query_rows, key_block, preferred_element_type=j...]
    ppermute x0 -> x25, waiting for transfers between devices: none -> 25.6 us  [send(): return lax.ppermute(value, AXES, routes(step))]
    reduce_sum x3 -> x0, other arithmetic: 6.5 us -> none  [the longest x1 4.95 us: update(): new_sum = jnp.sum(weights, axis=2)]
    pallas_call x0 -> x1, local copies, waits for them, and re-layouts: none -> 6.41 us  [split_columns(): pl.pallas_call(columns_kernel, grid=(8,), out_shape=(jax.ShapeDtypeStruct...]
  transfers between devices with their start and end apart: 2 -> 25, of which waited for: 2 -> 12; matrix products, arithmetic and copies ran while one was open for 2% -> 10% of each run, Pallas kernels for 0% -> 16%
where the time goes in v1:
time: 141 us; the launch traced here: 140 us
  starting transfers between devices  52.5 us (37%)
  Pallas kernels  39.1 us (28%)
  waiting for transfers between devices  25.6 us (18%)
  local copies, waits for them, and re-layouts  20.5 us (15%)
  other arithmetic  2.18 us (2%)
    ppermute x25, starting transfers between devices, send(): return lax.ppermute(value, AXES, routes(step))  52.5 us
    ppermute x25, waiting for transfers between devices, send(): return lax.ppermute(value, AXES, routes(step))  25.6 us
    pallas_call x1, Pallas kernels, attend(): pl.pallas_call(attend_kernel, out_shape=jax.ShapeDtypeStruct((2 * SPAN, H...  17.6 us
    pallas_call x1, Pallas kernels, split_columns(): pl.pallas_call(columns_kernel, grid=(8,), out_shape=(jax.ShapeDtypeStruct...  9.46 us
    pallas_call x1, Pallas kernels, project(): pl.pallas_call(project_kernel, out_shape=(jax.ShapeDtypeStruct((rows, 448...  6.79 us
    pallas_call x1, local copies, waits for them, and re-layouts, split_columns(): pl.pallas_call(columns_kernel, grid=(8,), out_shape=(jax.ShapeDtypeStruct...  6.41 us
    ppermute x1, local copies, waits for them, and re-layouts, send(): return lax.ppermute(value, AXES, routes(step))  6.35 us
    unnamed x43, local copies, waits for them, and re-layouts  6.2 us
  transfers between devices with their start and end apart: 25, of which 12 were waited for; matrix products, arithmetic and copies ran while one was open for 10% of the time, Pallas kernels for 16%

profile of v1, /device:TPU:1, one launch (start us, length us, event | category | flops | bytes accessed | tf_op | source)
XLA Modules:
  0.0 140.1 jit_solution(2414831620695855554)
XLA Ops:
  0.0 9.5 %split_columns.1 = (bf16[8,512,448]{2,1,0:T(8,128)(2,1)}, bf16[8,512,448]{2,1,0:T(8,128)(2,1)}) custom-call(bf16[512,7168]{1,0:T(8,128)(2,1)} %weight_ref.1), custom_call_target="tpu_custom_call" | custom-call | bytes 15000000 | tf_op jit(solution)/shard_map/split_columns/pallas_call | solution.py:338
  9.5 6.4 %copy.14 = bf16[8,512,448]{1,2,0:T(8,128)(2,1)} copy(bf16[8,512,448]{2,1,0:T(8,128)(2,1)} %get-tuple-element.22) | data formatting | bytes 7340032 | tf_op jit(solution)/shard_map/split_columns/pallas_call | solution.py:338
  15.9 3.3 %collective-permute-start.17 = (bf16[8,512,448]{1,2,0:T(8,128)(2,1)}, bf16[8,512,448]{1,2,0:T(8,128)(2,1)}, u32[]{:S(2)}, u32[]{:S(2)}) collective-permute-start(bf16[8,512,448]{1,2,0:T(8,128)(2,1)} %copy.14), channel_id=1, source_target_pairs={{0,1},{1,0},{16,17},{17,16},{32,33},{33,32},{48,49},{49,48},{64,65... | collective-permute-start | bytes 11010056 | tf_op jit(solution)/shard_map/ppermute | solution.py:45
  20.1 2.3 %pack_keys.1 = (bf16[2,144,512]{2,1,0:T(8,128)(2,1)}, bf16[144,512]{1,0:T(8,128)(2,1)}, bf16[144,512]{1,0:T(8,128)(2,1)}) custom-call(s32[32]{0:T(128)} %order_ref.5, bf16[256,576]{1,0:T(8,128)(2,1)} %copy.13.cache_ref, f32[160,128]{1,0:T(8,128)} %constant.22.clone.table_ref, bf16[64,64]{1,0:T(8,128)(2,1)} %constant.23.clone.swapper_ref), custom_call_target="tpu_custom_call" | custom-call | tf_op jit(solution)/shard_map/pack_keys/pallas_call | solution.py:138
  22.4 4.7 %collective-permute-start.6 = (bf16[144,512]{1,0:T(8,128)(2,1)}, bf16[144,512]{1,0:T(8,128)(2,1)S(1)}, u32[]{:S(2)}, u32[]{:S(2)}) collective-permute-start(bf16[144,512]{1,0:T(8,128)(2,1)} %get-tuple-element.20), channel_id=1, source_target_pairs={{0,48},{1,81},{16,64},{17,97},{32,80},{33,113},{48,96},{49,1},{64,... | collective-permute-start | bytes 442376 | tf_op jit(solution)/shard_map/ppermute | solution.py:45
  27.9 2.5 %collective-permute-start = (bf16[144,512]{1,0:T(8,128)(2,1)}, bf16[144,512]{1,0:T(8,128)(2,1)S(1)}, u32[]{:S(2)}, u32[]{:S(2)}) collective-permute-start(bf16[144,512]{1,0:T(8,128)(2,1)} %get-tuple-element.19), channel_id=1, source_target_pairs={{0,128},{1,137},{16,144},{17,153},{32,160},{33,169},{48,176},{49,1... | collective-permute-start | bytes 442376 | tf_op jit(solution)/shard_map/ppermute | solution.py:45
  32.8 4.5 %collective-permute-start.10 = (bf16[144,256]{1,0:T(8,128)(2,1)S(1)}, bf16[144,256]{1,0:T(8,128)(2,1)S(1)}, u32[]{:S(2)}, u32[]{:S(2)}) collective-permute-start(bf16[144,256]{1,0:T(8,128)(2,1)S(1)} %slice_select_fusion), channel_id=1, source_target_pairs={{0,64},{1,65},{16,80},{17,81},{32,96},{33,97},{48,112},{49,113},{6... | collective-permute-start | bytes 221192 | tf_op jit(solution)/shard_map/ppermute | solution.py:45
  39.6 2.7 %collective-permute-start.3 = (bf16[288,512]{1,0:T(8,128)(2,1)S(1)}, bf16[288,512]{1,0:T(8,128)(2,1)S(1)}, u32[]{:S(2)}, u32[]{:S(2)}) collective-permute-start(bf16[288,512]{1,0:T(8,128)(2,1)S(1)} %get-tuple-element.32.b12), channel_id=1, source_target_pairs={{0,2},{1,7},{16,18},{17,23},{32,34},{33,39},{48,50},{49,55},{64,66... | collective-permute-start | bytes 884744 | tf_op jit(solution)/shard_map/ppermute | solution.py:45
  42.9 4.1 %collective-permute-start.13 = (bf16[144,256]{1,0:T(8,128)(2,1)S(1)}, bf16[144,256]{1,0:T(8,128)(2,1)S(1)}, u32[]{:S(2)}, u32[]{:S(2)}) collective-permute-start(bf16[144,256]{1,0:T(8,128)(2,1)S(1)} %collective-permute-done.10.b4), channel_id=1, source_target_pairs={{0,130},{1,143},{16,146},{17,159},{32,162},{33,175},{48,178},{49,1... | collective-permute-start | bytes 221192 | tf_op jit(solution)/shard_map/ppermute | solution.py:45
  48.4 6.1 %collective-permute-start.5 = (bf16[288,512]{1,0:T(8,128)(2,1)S(1)}, bf16[288,512]{1,0:T(8,128)(2,1)S(1)}, u32[]{:S(2)}, u32[]{:S(2)}) collective-permute-start(bf16[288,512]{1,0:T(8,128)(2,1)S(1)} %get-tuple-element.32.b12), channel_id=1, source_target_pairs={{0,130},{1,143},{16,146},{17,159},{32,162},{33,175},{48,178},{49,1... | collective-permute-start | bytes 884744 | tf_op jit(solution)/shard_map/ppermute | solution.py:45
  58.2 5.2 %collective-permute-start.9 = (bf16[144,512]{1,0:T(8,128)(2,1)S(1)}, bf16[144,512]{1,0:T(8,128)(2,1)S(1)}, u32[]{:S(2)}, u32[]{:S(2)}) collective-permute-start(bf16[144,512]{1,0:T(8,128)(2,1)S(1)} %collective-permute-done.6.b3), channel_id=1, source_target_pairs={{0,130},{1,143},{16,146},{17,159},{32,162},{33,175},{48,178},{49,1... | collective-permute-start | bytes 442376 | tf_op jit(solution)/shard_map/ppermute | solution.py:45
  65.9 2.8 %collective-permute-done.11.y4 = bf16[144,256]{1,0:T(8,128)(2,1)S(1)} collective-permute-done((bf16[144,256]{1,0:T(8,128)(2,1)S(1)}, bf16[144,256]{1,0:T(8,128)(2,1)S(1)}, u32[]{:S(2)}, u32[]{:S(2)}) %collective-permute-start.11) | collective-permute-done | bytes 73760 | tf_op jit(solution)/shard_map/ppermute | solution.py:45
  68.9 4.9 %collective-permute-start.15 = (bf16[864,512]{1,0:T(8,128)(2,1)S(1)}, bf16[864,512]{1,0:T(8,128)(2,1)}, u32[]{:S(2)}, u32[]{:S(2)}) collective-permute-start(bf16[864,512]{1,0:T(8,128)(2,1)S(1)} %maximum_dynamic-update-slice_fusion), channel_id=1, source_target_pairs={{0,1},{1,0},{16,17},{17,16},{32,33},{33,32},{48,49},{49,48},{64,65... | collective-permute-start | bytes 2654216 | tf_op jit(solution)/shard_map/ppermute | solution.py:45
  74.7 2.9 %absorb_queries.1.q_ref = bf16[2,512,640]{2,1,0:T(8,128)(2,1)} custom-call(s32[32]{0:T(128)} %order_ref.5, bf16[4,256,192]{2,1,0:T(8,128)(2,1)} %bitcast.1, bf16[4,128,512]{2,1,0:T(8,128)(2,1)} %absorb_ref.1, f32[160,128]{1,0:T(8,128)} %constant.22.clone.table_ref, bf16[64,64]{1,0:T(8,128)(2,1)} %constant.23.clone.swapper_ref), custom_call_target="tpu_custom_call" | custom-call | tf_op jit(solution)/shard_map/absorb_queries/pallas_call | solution.py:168
  77.7 17.6 %attend.1.own_ref = bf16[256,512]{1,0:T(8,128)(2,1)} custom-call(s32[32]{0:T(128)} %order_ref.5, bf16[2,512,640]{2,1,0:T(8,128)(2,1)} %absorb_queries.1.q_ref, bf16[4,512,128]{2,1,0:T(8,128)(2,1)} %va_ref.1, bf16[2,144,512]{2,1,0:T(8,128)(2,1)} %get-tuple-element.18.own, bf16[144,512]{1,0:T(8,128)(2,1)} %copy-done.7, bf16[288,512]{1,0:T(8,128)(2,1)} %copy-done.11, ...), custom_call_target="tpu_custom_call" | custom-call | flops 6000000000 | bytes 8000000 | tf_op jit(solution)/shard_map/attend/pallas_call | solution.py:300
  95.4 6.4 %copy.15.got_ref = bf16[8,512,448]{2,1,0:T(8,128)(2,1)} copy(bf16[8,512,448]{1,2,0:T(8,128)(2,1)} %collective-permute-done.17) | data formatting | bytes 7340032 | tf_op jit(solution)/shard_map/ppermute | solution.py:45
  102.5 6.8 %project.1 = (bf16[256,448]{1,0:T(8,128)(2,1)}, bf16[256,448]{1,0:T(8,128)(2,1)}, bf16[256,448]{1,0:T(8,128)(2,1)}, bf16[256,448]{1,0:T(8,128)(2,1)}, bf16[256,4...) custom-call(bf16[256,512]{1,0:T(8,128)(2,1)} %attend.1.own_ref, ...), custom_call_target="tpu_custom_call" | custom-call | flops 1900000000 | bytes 8000000 | tf_op jit(solution)/shard_map/project/pallas_call | solution.py:377
  109.4 2.3 %collective-permute-start.19 = (bf16[256,448]{1,0:T(8,128)(2,1)}, bf16[256,448]{1,0:T(8,128)(2,1)S(1)}, u32[]{:S(2)}, u32[]{:S(2)}) collective-permute-start(bf16[256,448]{1,0:T(8,128)(2,1)} %get-tuple-element.24), channel_id=1, source_target_pairs={{0,10},{1,11},{16,26},{17,27},{32,42},{33,43},{48,58},{49,59},{64,... | collective-permute-start | bytes 688136 | tf_op jit(solution)/shard_map/ppermute | solution.py:45
  111.7 2.8 %collective-permute-start.20 = (bf16[256,448]{1,0:T(8,128)(2,1)}, bf16[256,448]{1,0:T(8,128)(2,1)S(1)}, u32[]{:S(2)}, u32[]{:S(2)}) collective-permute-start(bf16[256,448]{1,0:T(8,128)(2,1)} %get-tuple-element.25), channel_id=1, source_target_pairs={{0,14},{1,15},{16,30},{17,31},{32,46},{33,47},{48,62},{49,63},{64,... | collective-permute-start | bytes 688136 | tf_op jit(solution)/shard_map/ppermute | solution.py:45
  114.6 2.5 %collective-permute-start.21 = (bf16[256,448]{1,0:T(8,128)(2,1)}, bf16[256,448]{1,0:T(8,128)(2,1)S(1)}, u32[]{:S(2)}, u32[]{:S(2)}) collective-permute-start(bf16[256,448]{1,0:T(8,128)(2,1)} %get-tuple-element.26), channel_id=1, source_target_pairs={{0,4},{1,5},{16,20},{17,21},{32,36},{33,37},{48,52},{49,53},{64,68... | collective-permute-start | bytes 688136 | tf_op jit(solution)/shard_map/ppermute | solution.py:45
  118.9 3.2 %collective-permute-done.18 = bf16[256,448]{1,0:T(8,128)(2,1)S(1)} collective-permute-done((bf16[256,448]{1,0:T(8,128)(2,1)}, bf16[256,448]{1,0:T(8,128)(2,1)S(1)}, u32[]{:S(2)}, u32[]{:S(2)}) %collective-permute-start.18) | collective-permute-done | bytes 229408 | tf_op jit(solution)/shard_map/ppermute | solution.py:45
  122.1 4.2 %collective-permute-done.19 = bf16[256,448]{1,0:T(8,128)(2,1)S(1)} collective-permute-done((bf16[256,448]{1,0:T(8,128)(2,1)}, bf16[256,448]{1,0:T(8,128)(2,1)S(1)}, u32[]{:S(2)}, u32[]{:S(2)}) %collective-permute-start.19) | collective-permute-done | bytes 229408 | tf_op jit(solution)/shard_map/ppermute | solution.py:45
  129.2 4.3 %collective-permute-done.21 = bf16[256,448]{1,0:T(8,128)(2,1)S(1)} collective-permute-done((bf16[256,448]{1,0:T(8,128)(2,1)}, bf16[256,448]{1,0:T(8,128)(2,1)S(1)}, u32[]{:S(2)}, u32[]{:S(2)}) %collective-permute-start.21) | collective-permute-done | bytes 229408 | tf_op jit(solution)/shard_map/ppermute | solution.py:45
  134.6 3.4 %collective-permute-done.23 = bf16[256,448]{1,0:T(8,128)(2,1)S(1)} collective-permute-done((bf16[256,448]{1,0:T(8,128)(2,1)}, bf16[256,448]{1,0:T(8,128)(2,1)S(1)}, u32[]{:S(2)}, u32[]{:S(2)}) %collective-permute-start.23) | collective-permute-done | bytes 229408 | tf_op jit(solution)/shard_map/ppermute | solution.py:45
  (82 shorter events, 24.2 us)
Async XLA Ops:
  15.9 79.5 %collective-permute-start.17 = (bf16[8,512,448]{1,2,0:T(8,128)(2,1)}, bf16[8,512,448]{1,2,0:T(8,128)(2,1)}, u32[]{:S(2)}, u32[]{:S(2)}) collective-permute-start(bf16[8,512,448]{1,2,0:T(8,128)(2,1)} %copy.14), channel_id=1, source_target_pairs={{0,1},{1,0},{16,17},{17,16},{32,33},{33,32},{48,49},{49,48},{64,65... | collective-permute-start | bytes 11010056 | tf_op jit(solution)/shard_map/ppermute | solution.py:45
  22.4 20.0 %collective-permute-start.6 = (bf16[144,512]{1,0:T(8,128)(2,1)}, bf16[144,512]{1,0:T(8,128)(2,1)S(1)}, u32[]{:S(2)}, u32[]{:S(2)}) collective-permute-start(bf16[144,512]{1,0:T(8,128)(2,1)} %get-tuple-element.20), channel_id=1, source_target_pairs={{0,48},{1,81},{16,64},{17,97},{32,80},{33,113},{48,96},{49,1},{64,... | collective-permute-start | bytes 442376 | tf_op jit(solution)/shard_map/ppermute | solution.py:45
  27.2 11.8 %collective-permute-start.2 = (bf16[144,512]{1,0:T(8,128)(2,1)}, bf16[144,512]{1,0:T(8,128)(2,1)S(1)}, u32[]{:S(2)}, u32[]{:S(2)}) collective-permute-start(bf16[144,512]{1,0:T(8,128)(2,1)} %get-tuple-element.20), channel_id=1, source_target_pairs={{0,32},{1,97},{16,48},{17,113},{32,64},{33,1},{48,80},{49,17},{64,... | collective-permute-start | bytes 442376 | tf_op jit(solution)/shard_map/ppermute | solution.py:45
  27.4 10.9 %collective-permute-start.1 = (bf16[144,512]{1,0:T(8,128)(2,1)}, bf16[144,512]{1,0:T(8,128)(2,1)S(1)}, u32[]{:S(2)}, u32[]{:S(2)}) collective-permute-start(bf16[144,512]{1,0:T(8,128)(2,1)} %get-tuple-element.20), channel_id=1, source_target_pairs={{0,16},{1,113},{16,32},{17,1},{32,48},{33,17},{48,64},{49,33},{64,... | collective-permute-start | bytes 442376 | tf_op jit(solution)/shard_map/ppermute | solution.py:45
  27.9 4.9 %collective-permute-start = (bf16[144,512]{1,0:T(8,128)(2,1)}, bf16[144,512]{1,0:T(8,128)(2,1)S(1)}, u32[]{:S(2)}, u32[]{:S(2)}) collective-permute-start(bf16[144,512]{1,0:T(8,128)(2,1)} %get-tuple-element.19), channel_id=1, source_target_pairs={{0,128},{1,137},{16,144},{17,153},{32,160},{33,169},{48,176},{49,1... | collective-permute-start | bytes 442376 | tf_op jit(solution)/shard_map/ppermute | solution.py:45
  32.8 10.1 %collective-permute-start.10 = (bf16[144,256]{1,0:T(8,128)(2,1)S(1)}, bf16[144,256]{1,0:T(8,128)(2,1)S(1)}, u32[]{:S(2)}, u32[]{:S(2)}) collective-permute-start(bf16[144,256]{1,0:T(8,128)(2,1)S(1)} %slice_select_fusion), channel_id=1, source_target_pairs={{0,64},{1,65},{16,80},{17,81},{32,96},{33,97},{48,112},{49,113},{6... | collective-permute-start | bytes 221192 | tf_op jit(solution)/shard_map/ppermute | solution.py:45
  39.6 14.9 %collective-permute-start.3 = (bf16[288,512]{1,0:T(8,128)(2,1)S(1)}, bf16[288,512]{1,0:T(8,128)(2,1)S(1)}, u32[]{:S(2)}, u32[]{:S(2)}) collective-permute-start(bf16[288,512]{1,0:T(8,128)(2,1)S(1)} %get-tuple-element.32.b12), channel_id=1, source_target_pairs={{0,2},{1,7},{16,18},{17,23},{32,34},{33,39},{48,50},{49,55},{64,66... | collective-permute-start | bytes 884744 | tf_op jit(solution)/shard_map/ppermute | solution.py:45
  42.4 6.0 %collective-permute-start.7 = (bf16[144,512]{1,0:T(8,128)(2,1)S(1)}, bf16[144,512]{1,0:T(8,128)(2,1)S(1)}, u32[]{:S(2)}, u32[]{:S(2)}) collective-permute-start(bf16[144,512]{1,0:T(8,128)(2,1)S(1)} %collective-permute-done.6.b3), channel_id=1, source_target_pairs={{0,2},{1,7},{16,18},{17,23},{32,34},{33,39},{48,50},{49,55},{64,66... | collective-permute-start | bytes 442376 | tf_op jit(solution)/shard_map/ppermute | solution.py:45
  42.9 26.0 %collective-permute-start.13 = (bf16[144,256]{1,0:T(8,128)(2,1)S(1)}, bf16[144,256]{1,0:T(8,128)(2,1)S(1)}, u32[]{:S(2)}, u32[]{:S(2)}) collective-permute-start(bf16[144,256]{1,0:T(8,128)(2,1)S(1)} %collective-permute-done.10.b4), channel_id=1, source_target_pairs={{0,130},{1,143},{16,146},{17,159},{32,162},{33,175},{48,178},{49,1... | collective-permute-start | bytes 221192 | tf_op jit(solution)/shard_map/ppermute | solution.py:45
  47.0 9.7 %collective-permute-start.4 = (bf16[288,512]{1,0:T(8,128)(2,1)S(1)}, bf16[288,512]{1,0:T(8,128)(2,1)S(1)}, u32[]{:S(2)}, u32[]{:S(2)}) collective-permute-start(bf16[288,512]{1,0:T(8,128)(2,1)S(1)} %get-tuple-element.32.b12), channel_id=1, source_target_pairs={{0,128},{1,137},{16,144},{17,153},{32,160},{33,169},{48,176},{49,1... | collective-permute-start | bytes 884744 | tf_op jit(solution)/shard_map/ppermute | solution.py:45
  48.4 9.8 %collective-permute-start.5 = (bf16[288,512]{1,0:T(8,128)(2,1)S(1)}, bf16[288,512]{1,0:T(8,128)(2,1)S(1)}, u32[]{:S(2)}, u32[]{:S(2)}) collective-permute-start(bf16[288,512]{1,0:T(8,128)(2,1)S(1)} %get-tuple-element.32.b12), channel_id=1, source_target_pairs={{0,130},{1,143},{16,146},{17,159},{32,162},{33,175},{48,178},{49,1... | collective-permute-start | bytes 884744 | tf_op jit(solution)/shard_map/ppermute | solution.py:45
  54.6 14.2 %collective-permute-start.12 = (bf16[144,256]{1,0:T(8,128)(2,1)S(1)}, bf16[144,256]{1,0:T(8,128)(2,1)S(1)}, u32[]{:S(2)}, u32[]{:S(2)}) collective-permute-start(bf16[144,256]{1,0:T(8,128)(2,1)S(1)} %collective-permute-done.10.b4), channel_id=1, source_target_pairs={{0,128},{1,137},{16,144},{17,153},{32,160},{33,169},{48,176},{49,1... | collective-permute-start | bytes 221192 | tf_op jit(solution)/shard_map/ppermute | solution.py:45
  56.7 7.5 %collective-permute-start.8 = (bf16[144,512]{1,0:T(8,128)(2,1)S(1)}, bf16[144,512]{1,0:T(8,128)(2,1)S(1)}, u32[]{:S(2)}, u32[]{:S(2)}) collective-permute-start(bf16[144,512]{1,0:T(8,128)(2,1)S(1)} %collective-permute-done.6.b3), channel_id=1, source_target_pairs={{0,128},{1,137},{16,144},{17,153},{32,160},{33,169},{48,176},{49,1... | collective-permute-start | bytes 442376 | tf_op jit(solution)/shard_map/ppermute | solution.py:45
  58.2 7.3 %collective-permute-start.9 = (bf16[144,512]{1,0:T(8,128)(2,1)S(1)}, bf16[144,512]{1,0:T(8,128)(2,1)S(1)}, u32[]{:S(2)}, u32[]{:S(2)}) collective-permute-start(bf16[144,512]{1,0:T(8,128)(2,1)S(1)} %collective-permute-done.6.b3), channel_id=1, source_target_pairs={{0,130},{1,143},{16,146},{17,159},{32,162},{33,175},{48,178},{49,1... | collective-permute-start | bytes 442376 | tf_op jit(solution)/shard_map/ppermute | solution.py:45
  64.2 13.4 %collective-permute-start.14 = (bf16[1296,512]{1,0:T(8,128)(2,1)}, bf16[1296,512]{1,0:T(8,128)(2,1)}, u32[]{:S(2)}, u32[]{:S(2)}) collective-permute-start(bf16[1296,512]{1,0:T(8,128)(2,1)} %constant_dynamic-update-slice_fusion.2), channel_id=1, source_target_pairs={{0,1},{1,0},{16,17},{17,16},{32,33},{33,32},{48,49},{49,48},{64,65... | collective-permute-start | bytes 3981320 | tf_op jit(solution)/shard_map/ppermute | solution.py:45
  68.9 8.8 %collective-permute-start.15 = (bf16[864,512]{1,0:T(8,128)(2,1)S(1)}, bf16[864,512]{1,0:T(8,128)(2,1)}, u32[]{:S(2)}, u32[]{:S(2)}) collective-permute-start(bf16[864,512]{1,0:T(8,128)(2,1)S(1)} %maximum_dynamic-update-slice_fusion), channel_id=1, source_target_pairs={{0,1},{1,0},{16,17},{17,16},{32,33},{33,32},{48,49},{49,48},{64,65... | collective-permute-start | bytes 2654216 | tf_op jit(solution)/shard_map/ppermute | solution.py:45
  95.3 6.5 %collective-permute-start.16 = (bf16[256,512]{1,0:T(8,128)(2,1)}, bf16[256,512]{1,0:T(8,128)(2,1)S(1)}, u32[]{:S(2)}, u32[]{:S(2)}) collective-permute-start(bf16[256,512]{1,0:T(8,128)(2,1)} %attend.1.own_ref), channel_id=1, source_target_pairs={{0,1},{1,0},{16,17},{17,16},{32,33},{33,32},{48,49},{49,48},{64,65... | collective-permute-start | bytes 786440 | tf_op jit(solution)/shard_map/ppermute | solution.py:45
  109.3 12.8 %collective-permute-start.18 = (bf16[256,448]{1,0:T(8,128)(2,1)}, bf16[256,448]{1,0:T(8,128)(2,1)S(1)}, u32[]{:S(2)}, u32[]{:S(2)}) collective-permute-start(bf16[256,448]{1,0:T(8,128)(2,1)} %get-tuple-element.23), channel_id=1, source_target_pairs={{0,12},{1,13},{16,28},{17,29},{32,44},{33,45},{48,60},{49,61},{64,... | collective-permute-start | bytes 688136 | tf_op jit(solution)/shard_map/ppermute | solution.py:45
  109.4 17.0 %collective-permute-start.19 = (bf16[256,448]{1,0:T(8,128)(2,1)}, bf16[256,448]{1,0:T(8,128)(2,1)S(1)}, u32[]{:S(2)}, u32[]{:S(2)}) collective-permute-start(bf16[256,448]{1,0:T(8,128)(2,1)} %get-tuple-element.24), channel_id=1, source_target_pairs={{0,10},{1,11},{16,26},{17,27},{32,42},{33,43},{48,58},{49,59},{64,... | collective-permute-start | bytes 688136 | tf_op jit(solution)/shard_map/ppermute | solution.py:45
  111.7 17.4 %collective-permute-start.20 = (bf16[256,448]{1,0:T(8,128)(2,1)}, bf16[256,448]{1,0:T(8,128)(2,1)S(1)}, u32[]{:S(2)}, u32[]{:S(2)}) collective-permute-start(bf16[256,448]{1,0:T(8,128)(2,1)} %get-tuple-element.25), channel_id=1, source_target_pairs={{0,14},{1,15},{16,30},{17,31},{32,46},{33,47},{48,62},{49,63},{64,... | collective-permute-start | bytes 688136 | tf_op jit(solution)/shard_map/ppermute | solution.py:45
  114.6 18.9 %collective-permute-start.21 = (bf16[256,448]{1,0:T(8,128)(2,1)}, bf16[256,448]{1,0:T(8,128)(2,1)S(1)}, u32[]{:S(2)}, u32[]{:S(2)}) collective-permute-start(bf16[256,448]{1,0:T(8,128)(2,1)} %get-tuple-element.26), channel_id=1, source_target_pairs={{0,4},{1,5},{16,20},{17,21},{32,36},{33,37},{48,52},{49,53},{64,68... | collective-permute-start | bytes 688136 | tf_op jit(solution)/shard_map/ppermute | solution.py:45
  117.1 17.5 %collective-permute-start.22 = (bf16[256,448]{1,0:T(8,128)(2,1)}, bf16[256,448]{1,0:T(8,128)(2,1)S(1)}, u32[]{:S(2)}, u32[]{:S(2)}) collective-permute-start(bf16[256,448]{1,0:T(8,128)(2,1)} %get-tuple-element.27), channel_id=1, source_target_pairs={{0,8},{1,9},{16,24},{17,25},{32,40},{33,41},{48,56},{49,57},{64,72... | collective-permute-start | bytes 688136 | tf_op jit(solution)/shard_map/ppermute | solution.py:45
  122.1 15.9 %collective-permute-start.23 = (bf16[256,448]{1,0:T(8,128)(2,1)}, bf16[256,448]{1,0:T(8,128)(2,1)S(1)}, u32[]{:S(2)}, u32[]{:S(2)}) collective-permute-start(bf16[256,448]{1,0:T(8,128)(2,1)} %get-tuple-element.28), channel_id=1, source_target_pairs={{0,2},{1,3},{16,18},{17,19},{32,34},{33,35},{48,50},{49,51},{64,66... | collective-permute-start | bytes 688136 | tf_op jit(solution)/shard_map/ppermute | solution.py:45
  126.4 11.7 %collective-permute-start.24 = (bf16[256,448]{1,0:T(8,128)(2,1)}, bf16[256,448]{1,0:T(8,128)(2,1)S(1)}, u32[]{:S(2)}, u32[]{:S(2)}) collective-permute-start(bf16[256,448]{1,0:T(8,128)(2,1)} %get-tuple-element.29), channel_id=1, source_target_pairs={{0,6},{1,7},{16,22},{17,23},{32,38},{33,39},{48,54},{49,55},{64,70... | collective-permute-start | bytes 688136 | tf_op jit(solution)/shard_map/ppermute | solution.py:45
  (17 other events, 246.2 us)

commit v2 on v1

v2 whole, which is shorter than its diff:
```python
import functools
import math

import jax
import jax.numpy as jnp
import numpy as np
from jax import lax
from jax.experimental import pallas as pl
from jax.experimental.pallas import tpu as pltpu
from jax.sharding import PartitionSpec as P

BF16 = jnp.bfloat16
F32 = jnp.float32
AXES = ("ctx", "head")
NXL, NZ, NXH, NY, NC = 2, 8, 2, 4, 2
SPAN = 128
LAT = 512
ROPE = 64
KEY = LAT + ROPE
HEADS = 4
NEG = -1e30
MIB = 1024 * 1024


def vmem(mib):
    return pltpu.CompilerParams(vmem_limit_bytes=mib * MIB)


def device(x, y, z, c):
    x, y, z = x % 4, y % NY, z % NZ
    return ((((x % 2) * NZ + z) * NXH + x // 2) * NY + y) * NC + c


def routes(step):
    pairs = []
    for x in range(4):
        for y in range(NY):
            for z in range(NZ):
                for c in range(NC):
                    pairs.append((device(x, y, z, c), device(*step(x, y, z, c))))
    return pairs


def way(c):
    return 1 - 2 * c


def send(value, step):
    return lax.ppermute(value, AXES, routes(step))


def along(dx=0, dy=0, dz=0):
    return lambda x, y, z, c: (x + dx * way(c), y + dy * way(c), z + dz * way(c), c)


def swap(x, y, z, c):
    return x, y, z, 1 - c


def tables():
    inverse = 10000.0 ** (-np.arange(ROPE // 2, dtype=np.float64) * 2.0 / ROPE)[:, None]
    rows = inverse * np.arange(SPAN, dtype=np.float64)[None, :]
    spans = inverse * SPAN * np.arange(SPAN, dtype=np.float64)[None, :]
    return jnp.asarray(np.stack([np.cos(rows), np.sin(rows), np.cos(spans), np.sin(spans)]).astype(np.float32))


def cos_sin(table_ref, span):
    here = lax.broadcasted_iota(jnp.int32, (ROPE // 2, SPAN), 1) == span
    cs = jnp.sum(jnp.where(here, table_ref[2], 0.0), axis=1, keepdims=True)
    ss = jnp.sum(jnp.where(here, table_ref[3], 0.0), axis=1, keepdims=True)
    cr, sr = table_ref[0], table_ref[1]
    return cr * cs - sr * ss, cr * ss + sr * cs


def rotated(values, cos, sin):
    front, back = values[0:32].astype(F32), values[32:64].astype(F32)
    return jnp.concatenate([front * cos - back * sin, front * sin + back * cos], axis=0)


def me():
    ctx, head = lax.axis_index("ctx"), lax.axis_index("head")
    return ctx // NZ, ctx % NZ, head // (NY * NC), (head // NC) % NY, head % NC


def span_of(order_ref, xl, z, half):
    ctx = xl * NZ + lax.rem(z + 2 * NZ, NZ)
    a, b = order_ref[2 * ctx], order_ref[2 * ctx + 1]
    return jnp.where(half == 0, jnp.minimum(a, b), jnp.maximum(a, b))


def own_rows(order_ref, half):
    ctx = lax.axis_index("ctx")
    swapped = (order_ref[2 * ctx] > order_ref[2 * ctx + 1]).astype(jnp.int32)
    return pl.multiple_of(SPAN * (swapped ^ half), SPAN)


SMEM_SPEC = pl.BlockSpec(memory_space=pltpu.SMEM)
VMEM_SPEC = pl.BlockSpec(memory_space=pltpu.VMEM)
ANY_SPEC = pl.BlockSpec(memory_space=pl.ANY)


def pack_kernel(order_ref, cache_ref, table_ref, own_ref, slice_ref, part_ref, first_ref):
    xl, z, xh, y, c = me()
    for half in range(2):
        tokens = pl.ds(own_rows(order_ref, half), SPAN)
        cos, sin = cos_sin(table_ref, span_of(order_ref, xl, z, half))
        own_ref[half, 0:LAT, :] = cache_ref[0:LAT, tokens]
        own_ref[half, LAT:KEY, :] = rotated(cache_ref[LAT:KEY, tokens], cos, sin).astype(BF16)
    slice_ref[...] = own_ref[y % 2]
    part_ref[...] = own_ref[y % 2, pl.ds(pl.multiple_of(c * (KEY // 2), 32), KEY // 2), :]
    first_ref[...] = own_ref[c]


def pack(order, cache, table):
    return pl.pallas_call(
        pack_kernel,
        out_shape=(
            jax.ShapeDtypeStruct((2, KEY, SPAN), BF16),
            jax.ShapeDtypeStruct((KEY, SPAN), BF16),
            jax.ShapeDtypeStruct((KEY // 2, SPAN), BF16),
            jax.ShapeDtypeStruct((KEY, SPAN), BF16),
        ),
        in_specs=[SMEM_SPEC, VMEM_SPEC, VMEM_SPEC],
        out_specs=(VMEM_SPEC,) * 4,
        compiler_params=vmem(16),
        name="pack_keys",
    )(order, cache, table)


def absorb_kernel(order_ref, query_ref, absorb_ref, table_ref, out_ref):
    xl, z, xh, y, c = me()
    for half in range(2):
        tokens = pl.ds(own_rows(order_ref, half), SPAN)
        cos, sin = cos_sin(table_ref, span_of(order_ref, xl, z, half))
        for h in range(HEADS):
            rows = slice(h * SPAN, (h + 1) * SPAN)
            nope = query_ref[h, 0:128, tokens].T
            part = jnp.dot(nope, absorb_ref[h], preferred_element_type=F32)
            out_ref[half, rows, 0:LAT] = part.astype(BF16)
            turned = rotated(query_ref[h, 128:192, tokens], cos, sin)
            out_ref[half, rows, LAT:KEY] = turned.T.astype(BF16)


def absorb(order, queries, key_absorb, table):
    return pl.pallas_call(
        absorb_kernel,
        out_shape=jax.ShapeDtypeStruct((2, HEADS * SPAN, KEY), BF16),
        in_specs=[SMEM_SPEC] + [VMEM_SPEC] * 3,
        out_specs=VMEM_SPEC,
        compiler_params=vmem(16),
        name="absorb_queries",
    )(order, queries, key_absorb, table)


BLOCK = 4
STEPS = 7


def attend_kernel(
    order_ref, q_ref, va_ref, own, first, first2, bb, yy, xx, dd, bb2, yy2, xx2, dd2,
    out_ref, keys, scores, peaks, total, acc, sems,
):
    xl, z, xh, y, c = me()
    s = y % 2
    w = 1 - 2 * c
    copies = []

    def fetch(src, dst):
        copy = pltpu.make_async_copy(src, dst, sems.at[len(copies)])
        copy.start()
        copies.append(copy)

    for half in range(2):
        fetch(own.at[half], keys.at[span_of(order_ref, xl, z, half)])
    fetch(first, keys.at[span_of(order_ref, 1 - xl, z, c)])
    fetch(first2, keys.at[span_of(order_ref, 1 - xl, z, 1 - c)])
    kinds = ((xl, s), (xl, 1 - s), (1 - xl, s), (1 - xl, 1 - s))
    for (px, ph), mine, other in zip(kinds, (bb, yy, xx, dd), (bb2, yy2, xx2, dd2)):
        for t in (1, 2, 3):
            rows = pl.ds((t - 1) * KEY, KEY)
            fetch(mine.at[rows], keys.at[span_of(order_ref, px, z - w * t, ph)])
            fetch(other.at[rows], keys.at[span_of(order_ref, px, z + w * t, ph)])
        far = span_of(order_ref, px, z + 4, ph)
        rows = pl.ds(3 * KEY, KEY // 2)
        fetch(mine.at[rows], keys.at[far, pl.ds(pl.multiple_of(KEY // 2 * c, 32), KEY // 2)])
        fetch(other.at[rows], keys.at[far, pl.ds(pl.multiple_of(KEY // 2 * (1 - c), 32), KEY // 2)])
    for copy in copies:
        copy.wait()

    lower = span_of(order_ref, xl, z, 0)
    upper = 31 - lower
    count = lower // BLOCK
    scale = math.log2(math.e) / math.sqrt(192.0)
    wide = BLOCK * SPAN

    def tokens(block, rows):
        return jnp.concatenate([keys[BLOCK * block + i, rows, :] for i in range(BLOCK)], axis=1)

    def score(half, block):
        latent = jnp.dot(q_ref[half, :, 0:LAT], tokens(block, slice(0, LAT)), preferred_element_type=F32)
        turned = jnp.dot(q_ref[half, :, LAT:KEY], tokens(block, slice(LAT, KEY)), preferred_element_type=F32)
        return latent + turned

    def widest(value):
        parts = [value[:, 128 * i : 128 * (i + 1)] for i in range(BLOCK)]
        return jnp.maximum(jnp.maximum(parts[0], parts[1]), jnp.maximum(parts[2], parts[3]))

    def place(i):
        half = (i >= count).astype(jnp.int32)
        return half, i - half * count

    for half, span in ((0, lower), (1, upper)):
        value = score(half, span // BLOCK)
        row = lax.broadcasted_iota(jnp.int32, value.shape, 0) % SPAN + (span % BLOCK) * SPAN
        column = lax.broadcasted_iota(jnp.int32, value.shape, 1)
        value = jnp.where(column <= row, value, NEG)
        scores[STEPS + half] = value
        peaks[STEPS + half] = widest(value)
    for i in range(STEPS):
        value = score(*place(i))
        scores[i] = value
        peaks[i] = widest(value)

    for half in range(2):
        top = peaks[STEPS + half]
        for i in range(STEPS):
            top = jnp.where(place(i)[0] == half, jnp.maximum(top, peaks[i]), top)
        top = jnp.max(top, axis=1, keepdims=True) * scale
        peaks[STEPS + half] = jnp.broadcast_to(top, top.shape[:1] + (128,))

    def weigh(i, half, block):
        top = peaks[STEPS + half]
        parts = [jnp.exp2(scores[i, :, 128 * j : 128 * (j + 1)] * scale - top) for j in range(BLOCK)]
        weights = jnp.concatenate([part.astype(BF16) for part in parts], axis=1)
        product = lax.dot_general(
            weights, tokens(block, slice(0, LAT)), (((1,), (1,)), ((), ())), preferred_element_type=F32
        )
        return (parts[0] + parts[1]) + (parts[2] + parts[3]), product

    for half, span in ((0, lower), (1, upper)):
        total[half], acc[half] = weigh(STEPS + half, half, span // BLOCK)
    for i in range(STEPS):
        half, block = place(i)
        some, product = weigh(i, half, block)
        total[half] += some
        acc[half] += product

    for half in range(2):
        rows = own_rows(order_ref, half)
        for h in range(HEADS):
            part = slice(h * SPAN, (h + 1) * SPAN)
            bottom = jnp.sum(total[half, part, :], axis=1, keepdims=True)
            context = (acc[half, part, :] / bottom).astype(BF16)
            value = jnp.dot(context, va_ref[h], preferred_element_type=F32)
            out_ref[pl.ds(rows, SPAN), h * 128 : (h + 1) * 128] = value.astype(BF16)


def attend(order, q, value_absorb, pieces):
    rows = HEADS * SPAN
    return pl.pallas_call(
        attend_kernel,
        out_shape=jax.ShapeDtypeStruct((2 * SPAN, HEADS * 128), BF16),
        in_specs=[SMEM_SPEC, VMEM_SPEC, VMEM_SPEC] + [ANY_SPEC] * len(pieces),
        out_specs=VMEM_SPEC,
        scratch_shapes=[
            pltpu.VMEM((32, KEY, SPAN), BF16),
            pltpu.VMEM((STEPS + 2, rows, BLOCK * SPAN), F32),
            pltpu.VMEM((STEPS + 2, rows, 128), F32),
            pltpu.VMEM((2, rows, 128), F32),
            pltpu.VMEM((2, rows, LAT), F32),
            pltpu.SemaphoreType.DMA((40,)),
        ],
        compiler_params=vmem(40),
        cost_estimate=pl.CostEstimate(flops=6_000_000_000, bytes_accessed=8_000_000, transcendentals=2_200_000),
        name="attend",
    )(order, q, value_absorb, *pieces)


def columns_kernel(weight_ref, wait_ref, keep_ref, give_ref):
    c = lax.axis_index("head") % NC
    turned = weight_ref[...].T

    @pl.when(c == 0)
    def _():
        keep_ref[...] = turned[0:448]
        give_ref[...] = turned[448:896]

    @pl.when(c == 1)
    def _():
        keep_ref[...] = turned[448:896]
        give_ref[...] = turned[0:448]


def split_columns(weight, wait):
    rows = weight.shape[0]
    return pl.pallas_call(
        columns_kernel,
        grid=(8,),
        out_shape=(jax.ShapeDtypeStruct((8 * 448, rows), BF16),) * 2,
        in_specs=[pl.BlockSpec((rows, 896), lambda k: (0, k)), ANY_SPEC],
        out_specs=(pl.BlockSpec((448, rows), lambda k: (k, 0)),) * 2,
        compiler_params=vmem(24),
        cost_estimate=pl.CostEstimate(flops=0, bytes_accessed=15_000_000, transcendentals=0),
        name="split_columns",
    )(weight, wait)


OFFSETS = [(1, 2), (1, 1), (1, 3), (0, 2), (1, 0), (0, 1), (0, 3), (0, 0)]


def project_kernel(own_ref, other_ref, keep_ref, got_ref, *outs):
    xl, z, xh, y, c = me()
    contract = (((1,), (1,)), ((), ()))
    for out_ref, (dx, dy) in zip(outs, OFFSETS):
        k = lax.rem(xh + dx, NXH) * NY + lax.rem(y + dy, NY)
        rows = pl.ds(pl.multiple_of(k * 448, 64), 448)
        term = lax.dot_general(keep_ref[rows, :], own_ref[...], contract, preferred_element_type=F32)
        term += lax.dot_general(got_ref[rows, :], other_ref[...], contract, preferred_element_type=F32)
        out_ref[...] = term.astype(BF16)


def project(own, other, keep, got):
    return pl.pallas_call(
        project_kernel,
        out_shape=(jax.ShapeDtypeStruct((448, 256), BF16),) * 8,
        in_specs=[VMEM_SPEC] * 4,
        out_specs=(VMEM_SPEC,) * 8,
        compiler_params=vmem(24),
        cost_estimate=pl.CostEstimate(flops=1_900_000_000, bytes_accessed=8_000_000, transcendentals=0),
        name="project",
    )(own, other, keep, got)


def body(queries, latent_cache, key_absorb, value_absorb, out_weight, span_order):
    table = tables()
    own, piece, part, first_half = pack(span_order, latent_cache.T, table)

    b1 = send(piece, along(dz=1))
    b2 = send(piece, along(dz=2))
    b3 = send(piece, along(dz=3))
    b4 = send(part, along(dz=4))
    first = send(first_half, along(dx=1))
    keep, give = split_columns(out_weight, piece)
    bb, give, first = lax.optimization_barrier((jnp.concatenate([b1, b2, b3, b4], axis=0), give, first))
    yy, xx, dd = (send(bb, step) for step in (along(dy=1), along(dx=1), along(dx=1, dy=1)))
    got = send(give, swap)
    bb2 = send(bb, swap)
    first2 = send(first, swap)
    q = absorb(span_order, queries.transpose(1, 2, 0), key_absorb, table)
    yy, q = lax.optimization_barrier((yy, q))
    yy2, xx2, dd2 = (send(value, swap) for value in (yy, xx, dd))

    values = attend(span_order, q, value_absorb, (own, first, first2, bb, yy, xx, dd, bb2, yy2, xx2, dd2))
    other = send(values, swap)
    terms = project(values, other, keep, got)
    landed = [
        term if (dx, dy) == (0, 0) else send(term, lambda x, y, z, c, dx=dx, dy=dy: (x + 2 * dx, y + dy, z, c))
        for term, (dx, dy) in zip(terms, OFFSETS)
    ]
    return functools.reduce(jnp.add, [term.astype(F32) for term in landed]).astype(BF16).T


def solution(mesh):
    return jax.shard_map(
        body,
        mesh=mesh,
        in_specs=(
            P("ctx", "head", None),
            P("ctx", None),
            P("head", None, None),
            P("head", None, None),
            P("head", None),
            P(),
        ),
        out_specs=P("ctx", "head"),
        check_vma=False,
    )
```

time: 141 us -> 96.4 us (0.68)
  Pallas kernels: 39.1 us -> 24 us
  local copies, waits for them, and re-layouts: 20.5 us -> 5.56 us
  starting transfers between devices: 52.5 us -> 37.7 us
  waiting for transfers between devices: 25.6 us -> 27.8 us
    ppermute x25 -> x22, starting transfers between devices: 52.5 us -> 37.7 us  [send(): return lax.ppermute(value, AXES, routes(step))]
    pallas_call x1 -> x0, local copies, waits for them, and re-layouts: 6.41 us -> none  [split_columns(): pl.pallas_call(columns_kernel, grid=(8,), out_shape=(jax.ShapeDtypeStruct...]
    ppermute x1 -> x0, local copies, waits for them, and re-layouts: 6.35 us -> none  [send(): return lax.ppermute(value, AXES, routes(step))]
    pallas_call x2, Pallas kernels: 9.1 us -> 2.81 us  [the longest x1 2.09 us: project(): pl.pallas_call(project_kernel, out_shape=(jax.ShapeDtypeStruct((448, 256)...]
    pallas_call x1, Pallas kernels: 9.46 us -> 3.6 us  [split_columns(): pl.pallas_call(columns_kernel, grid=(8,), out_shape=(jax.ShapeDtypeStruct...]
    ppermute x25 -> x22, waiting for transfers between devices: 25.6 us -> 27.8 us  [send(): return lax.ppermute(value, AXES, routes(step))]
    pallas_call x1, Pallas kernels: 2.87 us -> 1.02 us  [absorb(): pl.pallas_call(absorb_kernel, out_shape=jax.ShapeDtypeStruct((2, HEADS *...]
    unnamed x43 -> x18, local copies, waits for them, and re-layouts: 6.2 us -> 5.56 us
  transfers between devices with their start and end apart: 25 -> 22, of which waited for: 12 -> 11; matrix products, arithmetic and copies ran while one was open for 10% -> 0% of each run, Pallas kernels for 16% -> 22%
where the time goes in v2:
time: 96.4 us; the launch traced here: 96.2 us
  starting transfers between devices  37.7 us (39%)
  waiting for transfers between devices  27.8 us (29%)
  Pallas kernels  24 us (25%)
  local copies, waits for them, and re-layouts  5.56 us (6%)
    ppermute x22, starting transfers between devices, send(): return lax.ppermute(value, AXES, routes(step))  37.7 us
    ppermute x22, waiting for transfers between devices, send(): return lax.ppermute(value, AXES, routes(step))  27.8 us
    pallas_call x1, Pallas kernels, attend(): pl.pallas_call(attend_kernel, out_shape=jax.ShapeDtypeStruct((2 * SPAN, H...  16.6 us
    unnamed x18, local copies, waits for them, and re-layouts  5.56 us
    pallas_call x1, Pallas kernels, split_columns(): pl.pallas_call(columns_kernel, grid=(8,), out_shape=(jax.ShapeDtypeStruct...  3.6 us
    pallas_call x1, Pallas kernels, project(): pl.pallas_call(project_kernel, out_shape=(jax.ShapeDtypeStruct((448, 256)...  2.09 us
  transfers between devices with their start and end apart: 22, of which 11 were waited for; matrix products, arithmetic and copies ran while one was open for 0% of the time, Pallas kernels for 22%

profile of v2, /device:TPU:1, one launch (start us, length us, event | category | flops | bytes accessed | tf_op | source)
XLA Modules:
  0.0 96.2 jit_solution(8203097523446312577)
XLA Ops:
  3.2 7.4 %collective-permute-start.2 = (bf16[576,128]{1,0:T(8,128)(2,1)S(1)}, bf16[576,128]{1,0:T(8,128)(2,1)S(1)}, u32[]{:S(2)}, u32[]{:S(2)}) collective-permute-start(bf16[576,128]{1,0:T(8,128)(2,1)S(1)} %get-tuple-element.24.wait_ref), channel_id=1, source_target_pairs={{0,48},{1,81},{16,64},{17,97},{32,80},{33,113},{48,96},{49,1},{64,... | collective-permute-start | bytes 442376 | tf_op jit(solution)/shard_map/ppermute | solution.py:49
  11.3 4.5 %collective-permute-start.3 = (bf16[288,128]{1,0:T(8,128)(2,1)S(1)}, bf16[288,128]{1,0:T(8,128)(2,1)S(1)}, u32[]{:S(2)}, u32[]{:S(2)}) collective-permute-start(bf16[288,128]{1,0:T(8,128)(2,1)S(1)} %get-tuple-element.25), channel_id=1, source_target_pairs={{0,64},{1,65},{16,80},{17,81},{32,96},{33,97},{48,112},{49,113},{6... | collective-permute-start | bytes 221192 | tf_op jit(solution)/shard_map/ppermute | solution.py:49
  15.8 2.5 %collective-permute-start.4 = (bf16[576,128]{1,0:T(8,128)(2,1)S(1)}, bf16[576,128]{1,0:T(8,128)(2,1)S(1)}, u32[]{:S(2)}, u32[]{:S(2)}) collective-permute-start(bf16[576,128]{1,0:T(8,128)(2,1)S(1)} %get-tuple-element.27), channel_id=1, source_target_pairs={{0,128},{1,137},{16,144},{17,153},{32,160},{33,169},{48,176},{49,1... | collective-permute-start | bytes 442376 | tf_op jit(solution)/shard_map/ppermute | solution.py:49
  18.2 3.1 %copy-done = bf16[512,7168]{1,0:T(8,128)(2,1)S(1)} copy-done((bf16[512,7168]{1,0:T(8,128)(2,1)S(1)}, bf16[512,7168]{1,0:T(8,128)(2,1)}, u32[]{:S(2)}) %copy-start) | copy-done | bytes 7340056
  21.4 3.6 %split_columns.1 = (bf16[3584,512]{1,0:T(8,128)(2,1)S(1)}, bf16[3584,512]{1,0:T(8,128)(2,1)S(1)}) custom-call(bf16[512,7168]{1,0:T(8,128)(2,1)S(1)} %copy-done, bf16[576,128]{1,0:T(8,128)(2,1)S(1)} %get-tuple-element.24.wait_ref), custom_call_target="tpu_custom_call" | custom-call | bytes 15000000 | tf_op jit(solution)/shard_map/split_columns/pallas_call | solution.py:296
  25.1 2.4 %collective-permute-start.14 = (bf16[3584,512]{1,0:T(8,128)(2,1)S(1)}, bf16[3584,512]{1,0:T(8,128)(2,1)S(1)}, u32[]{:S(2)}, u32[]{:S(2)}) collective-permute-start(bf16[3584,512]{1,0:T(8,128)(2,1)S(1)} %get-tuple-element.34), channel_id=1, source_target_pairs={{0,1},{1,0},{16,17},{17,16},{32,33},{33,32},{48,49},{49,48},{64,65... | collective-permute-start | bytes 11010056 | tf_op jit(solution)/shard_map/ppermute | solution.py:49
  27.5 2.7 %collective-permute-start.5 = (bf16[2016,128]{1,0:T(8,128)(2,1)S(1)}, bf16[2016,128]{1,0:T(8,128)(2,1)S(1)}, u32[]{:S(2)}, u32[]{:S(2)}) collective-permute-start(bf16[2016,128]{1,0:T(8,128)(2,1)S(1)} %pad_maximum_fusion.bb), channel_id=1, source_target_pairs={{0,2},{1,7},{16,18},{17,23},{32,34},{33,39},{48,50},{49,55},{64,66... | collective-permute-start | bytes 1548296 | tf_op jit(solution)/shard_map/ppermute | solution.py:49
  30.2 2.7 %collective-permute-start.8 = (bf16[2016,128]{1,0:T(8,128)(2,1)S(1)}, bf16[2016,128]{1,0:T(8,128)(2,1)S(1)}, u32[]{:S(2)}, u32[]{:S(2)}) collective-permute-start(bf16[2016,128]{1,0:T(8,128)(2,1)S(1)} %pad_maximum_fusion.bb), channel_id=1, source_target_pairs={{0,130},{1,143},{16,146},{17,159},{32,162},{33,175},{48,178},{49,1... | collective-permute-start | bytes 1548296 | tf_op jit(solution)/shard_map/ppermute | solution.py:49
  34.5 7.3 %collective-permute-done.5.yy = bf16[2016,128]{1,0:T(8,128)(2,1)S(1)} collective-permute-done((bf16[2016,128]{1,0:T(8,128)(2,1)S(1)}, bf16[2016,128]{1,0:T(8,128)(2,1)S(1)}, u32[]{:S(2)}, u32[]{:S(2)}) %collective-permute-start.5) | collective-permute-done | bytes 516128 | tf_op jit(solution)/shard_map/ppermute | solution.py:49
  41.8 1.6 %collective-permute-start.9 = (bf16[2016,128]{1,0:T(8,128)(2,1)S(1)}, bf16[2016,128]{1,0:T(8,128)(2,1)S(1)}, u32[]{:S(2)}, u32[]{:S(2)}) collective-permute-start(bf16[2016,128]{1,0:T(8,128)(2,1)S(1)} %pad_maximum_fusion.bb), channel_id=1, source_target_pairs={{0,1},{1,0},{16,17},{17,16},{32,33},{33,32},{48,49},{49,48},{64,65... | collective-permute-start | bytes 1548296 | tf_op jit(solution)/shard_map/ppermute | solution.py:49
  44.5 1.5 %collective-permute-start.11 = (bf16[2016,128]{1,0:T(8,128)(2,1)S(1)}, bf16[2016,128]{1,0:T(8,128)(2,1)S(1)}, u32[]{:S(2)}, u32[]{:S(2)}) collective-permute-start(bf16[2016,128]{1,0:T(8,128)(2,1)S(1)} %collective-permute-done.7.xx), channel_id=1, source_target_pairs={{0,1},{1,0},{16,17},{17,16},{32,33},{33,32},{48,49},{49,48},{64,65... | collective-permute-start | bytes 1548296 | tf_op jit(solution)/shard_map/ppermute | solution.py:49
  46.0 1.5 %collective-permute-done.11.xx2 = bf16[2016,128]{1,0:T(8,128)(2,1)S(1)} collective-permute-done((bf16[2016,128]{1,0:T(8,128)(2,1)S(1)}, bf16[2016,128]{1,0:T(8,128)(2,1)S(1)}, u32[]{:S(2)}, u32[]{:S(2)}) %collective-permute-start.11) | collective-permute-done | bytes 516128 | tf_op jit(solution)/shard_map/ppermute | solution.py:49
  48.3 16.6 %attend.1.own_ref = bf16[256,512]{1,0:T(8,128)(2,1)S(1)} custom-call(s32[32]{0:T(128)S(1)} %copy-done.7, bf16[2,512,576]{2,1,0:T(8,128)(2,1)S(1)} %absorb_queries.1.q_ref, bf16[4,512,128]{2,1,0:T(8,128)(2,1)S(1)} %copy-done.8, bf16[2,576,128]{2,1,0:T(8,128)(2,1)S(1)} %get-tuple-element.30.own, bf16[576,128]{1,0:T(8,128)(2,1)S(1)} %collective-permute-done.4.first, ...), custom_call_target="tpu_custom_call" | custom-call | flops 6000000000 | bytes 8000000 | tf_op jit(solution)/shard_map/attend/pallas_call | solution.py:260
  66.5 2.1 %project.1 = (bf16[448,256]{1,0:T(8,128)(2,1)S(1)}, bf16[448,256]{1,0:T(8,128)(2,1)S(1)}, bf16[448,256]{1,0:T(8,128)(2,1)S(1)}, bf16[448,256]{1,0:T(8,128)(2,1)S...) custom-call(bf16[256,512]{1,0:T(8,128)(2,1)S(1)} %attend.1.own_ref, ...), custom_call_target="tpu_custom_call" | custom-call | flops 1900000000 | bytes 8000000 | tf_op jit(solution)/shard_map/project/pallas_call | solution.py:323
  68.6 3.1 %collective-permute-start.15 = (bf16[448,256]{1,0:T(8,128)(2,1)S(1)}, bf16[448,256]{1,0:T(8,128)(2,1)S(1)}, u32[]{:S(2)}, u32[]{:S(2)}) collective-permute-start(bf16[448,256]{1,0:T(8,128)(2,1)S(1)} %get-tuple-element.35), channel_id=1, source_target_pairs={{0,12},{1,13},{16,28},{17,29},{32,44},{33,45},{48,60},{49,61},{64,... | collective-permute-start | bytes 688136 | tf_op jit(solution)/shard_map/ppermute | solution.py:49
  71.7 1.4 %collective-permute-start.16 = (bf16[448,256]{1,0:T(8,128)(2,1)S(1)}, bf16[448,256]{1,0:T(8,128)(2,1)S(1)}, u32[]{:S(2)}, u32[]{:S(2)}) collective-permute-start(bf16[448,256]{1,0:T(8,128)(2,1)S(1)} %get-tuple-element.36), channel_id=1, source_target_pairs={{0,10},{1,11},{16,26},{17,27},{32,42},{33,43},{48,58},{49,59},{64,... | collective-permute-start | bytes 688136 | tf_op jit(solution)/shard_map/ppermute | solution.py:49
  73.1 3.7 %collective-permute-start.17 = (bf16[448,256]{1,0:T(8,128)(2,1)S(1)}, bf16[448,256]{1,0:T(8,128)(2,1)S(1)}, u32[]{:S(2)}, u32[]{:S(2)}) collective-permute-start(bf16[448,256]{1,0:T(8,128)(2,1)S(1)} %get-tuple-element.37), channel_id=1, source_target_pairs={{0,14},{1,15},{16,30},{17,31},{32,46},{33,47},{48,62},{49,63},{64,... | collective-permute-start | bytes 688136 | tf_op jit(solution)/shard_map/ppermute | solution.py:49
  76.9 1.4 %collective-permute-start.19 = (bf16[448,256]{1,0:T(8,128)(2,1)S(1)}, bf16[448,256]{1,0:T(8,128)(2,1)S(1)}, u32[]{:S(2)}, u32[]{:S(2)}) collective-permute-start(bf16[448,256]{1,0:T(8,128)(2,1)S(1)} %get-tuple-element.39), channel_id=1, source_target_pairs={{0,8},{1,9},{16,24},{17,25},{32,40},{33,41},{48,56},{49,57},{64,72... | collective-permute-start | bytes 688136 | tf_op jit(solution)/shard_map/ppermute | solution.py:49
  78.2 1.2 %collective-permute-done.15 = bf16[448,256]{1,0:T(8,128)(2,1)S(1)} collective-permute-done((bf16[448,256]{1,0:T(8,128)(2,1)S(1)}, bf16[448,256]{1,0:T(8,128)(2,1)S(1)}, u32[]{:S(2)}, u32[]{:S(2)}) %collective-permute-start.15) | collective-permute-done | bytes 229408 | tf_op jit(solution)/shard_map/ppermute | solution.py:49
  80.5 4.3 %collective-permute-done.16 = bf16[448,256]{1,0:T(8,128)(2,1)S(1)} collective-permute-done((bf16[448,256]{1,0:T(8,128)(2,1)S(1)}, bf16[448,256]{1,0:T(8,128)(2,1)S(1)}, u32[]{:S(2)}, u32[]{:S(2)}) %collective-permute-start.16) | collective-permute-done | bytes 229408 | tf_op jit(solution)/shard_map/ppermute | solution.py:49
  84.8 3.9 %collective-permute-done.17 = bf16[448,256]{1,0:T(8,128)(2,1)S(1)} collective-permute-done((bf16[448,256]{1,0:T(8,128)(2,1)S(1)}, bf16[448,256]{1,0:T(8,128)(2,1)S(1)}, u32[]{:S(2)}, u32[]{:S(2)}) %collective-permute-start.17) | collective-permute-done | bytes 229408 | tf_op jit(solution)/shard_map/ppermute | solution.py:49
  88.8 1.7 %collective-permute-done.18 = bf16[448,256]{1,0:T(8,128)(2,1)S(1)} collective-permute-done((bf16[448,256]{1,0:T(8,128)(2,1)S(1)}, bf16[448,256]{1,0:T(8,128)(2,1)S(1)}, u32[]{:S(2)}, u32[]{:S(2)}) %collective-permute-start.18) | collective-permute-done | bytes 229408 | tf_op jit(solution)/shard_map/ppermute | solution.py:49
  90.4 3.0 %collective-permute-done.19 = bf16[448,256]{1,0:T(8,128)(2,1)S(1)} collective-permute-done((bf16[448,256]{1,0:T(8,128)(2,1)S(1)}, bf16[448,256]{1,0:T(8,128)(2,1)S(1)}, u32[]{:S(2)}, u32[]{:S(2)}) %collective-permute-start.19) | collective-permute-done | bytes 229408 | tf_op jit(solution)/shard_map/ppermute | solution.py:49
  93.4 1.9 %collective-permute-done.20 = bf16[448,256]{1,0:T(8,128)(2,1)S(1)} collective-permute-done((bf16[448,256]{1,0:T(8,128)(2,1)S(1)}, bf16[448,256]{1,0:T(8,128)(2,1)S(1)}, u32[]{:S(2)}, u32[]{:S(2)}) %collective-permute-start.20) | collective-permute-done | bytes 229408 | tf_op jit(solution)/shard_map/ppermute | solution.py:49
  (45 shorter events, 11.0 us)
Async XLA Ops:
  3.2 21.8 %collective-permute-start.2 = (bf16[576,128]{1,0:T(8,128)(2,1)S(1)}, bf16[576,128]{1,0:T(8,128)(2,1)S(1)}, u32[]{:S(2)}, u32[]{:S(2)}) collective-permute-start(bf16[576,128]{1,0:T(8,128)(2,1)S(1)} %get-tuple-element.24.wait_ref), channel_id=1, source_target_pairs={{0,48},{1,81},{16,64},{17,97},{32,80},{33,113},{48,96},{49,1},{64,... | collective-permute-start | bytes 442376 | tf_op jit(solution)/shard_map/ppermute | solution.py:49
  10.6 14.4 %collective-permute-start.1 = (bf16[576,128]{1,0:T(8,128)(2,1)S(1)}, bf16[576,128]{1,0:T(8,128)(2,1)S(1)}, u32[]{:S(2)}, u32[]{:S(2)}) collective-permute-start(bf16[576,128]{1,0:T(8,128)(2,1)S(1)} %get-tuple-element.24.wait_ref), channel_id=1, source_target_pairs={{0,32},{1,97},{16,48},{17,113},{32,64},{33,1},{48,80},{49,17},{64,... | collective-permute-start | bytes 442376 | tf_op jit(solution)/shard_map/ppermute | solution.py:49
  10.8 14.2 %collective-permute-start = (bf16[576,128]{1,0:T(8,128)(2,1)S(1)}, bf16[576,128]{1,0:T(8,128)(2,1)S(1)}, u32[]{:S(2)}, u32[]{:S(2)}) collective-permute-start(bf16[576,128]{1,0:T(8,128)(2,1)S(1)} %get-tuple-element.24.wait_ref), channel_id=1, source_target_pairs={{0,16},{1,113},{16,32},{17,1},{32,48},{33,17},{48,64},{49,33},{64,... | collective-permute-start | bytes 442376 | tf_op jit(solution)/shard_map/ppermute | solution.py:49
  11.3 13.7 %collective-permute-start.3 = (bf16[288,128]{1,0:T(8,128)(2,1)S(1)}, bf16[288,128]{1,0:T(8,128)(2,1)S(1)}, u32[]{:S(2)}, u32[]{:S(2)}) collective-permute-start(bf16[288,128]{1,0:T(8,128)(2,1)S(1)} %get-tuple-element.25), channel_id=1, source_target_pairs={{0,64},{1,65},{16,80},{17,81},{32,96},{33,97},{48,112},{49,113},{6... | collective-permute-start | bytes 221192 | tf_op jit(solution)/shard_map/ppermute | solution.py:49
  15.8 9.3 %collective-permute-start.4 = (bf16[576,128]{1,0:T(8,128)(2,1)S(1)}, bf16[576,128]{1,0:T(8,128)(2,1)S(1)}, u32[]{:S(2)}, u32[]{:S(2)}) collective-permute-start(bf16[576,128]{1,0:T(8,128)(2,1)S(1)} %get-tuple-element.27), channel_id=1, source_target_pairs={{0,128},{1,137},{16,144},{17,153},{32,160},{33,169},{48,176},{49,1... | collective-permute-start | bytes 442376 | tf_op jit(solution)/shard_map/ppermute | solution.py:49
  21.3 12.1 %copy-start.7 = (s32[32]{0:T(128)S(1)}, s32[32]{0:T(128)}, u32[]{:S(2)}) copy-start(s32[32]{0:T(128)} %order_ref.5) | copy-start | bytes 388
  21.3 26.9 %copy-start.8 = (bf16[4,512,128]{2,1,0:T(8,128)(2,1)S(1)}, bf16[4,512,128]{2,1,0:T(8,128)(2,1)}, u32[]{:S(2)}) copy-start(bf16[4,512,128]{2,1,0:T(8,128)(2,1)} %va_ref.1) | copy-start | bytes 1572868
  25.1 41.5 %collective-permute-start.14 = (bf16[3584,512]{1,0:T(8,128)(2,1)S(1)}, bf16[3584,512]{1,0:T(8,128)(2,1)S(1)}, u32[]{:S(2)}, u32[]{:S(2)}) collective-permute-start(bf16[3584,512]{1,0:T(8,128)(2,1)S(1)} %get-tuple-element.34), channel_id=1, source_target_pairs={{0,1},{1,0},{16,17},{17,16},{32,33},{33,32},{48,49},{49,48},{64,65... | collective-permute-start | bytes 11010056 | tf_op jit(solution)/shard_map/ppermute | solution.py:49
  27.5 14.3 %collective-permute-start.5 = (bf16[2016,128]{1,0:T(8,128)(2,1)S(1)}, bf16[2016,128]{1,0:T(8,128)(2,1)S(1)}, u32[]{:S(2)}, u32[]{:S(2)}) collective-permute-start(bf16[2016,128]{1,0:T(8,128)(2,1)S(1)} %pad_maximum_fusion.bb), channel_id=1, source_target_pairs={{0,2},{1,7},{16,18},{17,23},{32,34},{33,39},{48,50},{49,55},{64,66... | collective-permute-start | bytes 1548296 | tf_op jit(solution)/shard_map/ppermute | solution.py:49
  30.2 13.2 %collective-permute-start.8 = (bf16[2016,128]{1,0:T(8,128)(2,1)S(1)}, bf16[2016,128]{1,0:T(8,128)(2,1)S(1)}, u32[]{:S(2)}, u32[]{:S(2)}) collective-permute-start(bf16[2016,128]{1,0:T(8,128)(2,1)S(1)} %pad_maximum_fusion.bb), channel_id=1, source_target_pairs={{0,130},{1,143},{16,146},{17,159},{32,162},{33,175},{48,178},{49,1... | collective-permute-start | bytes 1548296 | tf_op jit(solution)/shard_map/ppermute | solution.py:49
  32.9 11.6 %collective-permute-start.7 = (bf16[2016,128]{1,0:T(8,128)(2,1)S(1)}, bf16[2016,128]{1,0:T(8,128)(2,1)S(1)}, u32[]{:S(2)}, u32[]{:S(2)}) collective-permute-start(bf16[2016,128]{1,0:T(8,128)(2,1)S(1)} %pad_maximum_fusion.bb), channel_id=1, source_target_pairs={{0,128},{1,137},{16,144},{17,153},{32,160},{33,169},{48,176},{49,1... | collective-permute-start | bytes 1548296 | tf_op jit(solution)/shard_map/ppermute | solution.py:49
  33.4 12.6 %collective-permute-start.6 = (bf16[576,128]{1,0:T(8,128)(2,1)S(1)}, bf16[576,128]{1,0:T(8,128)(2,1)S(1)}, u32[]{:S(2)}, u32[]{:S(2)}) collective-permute-start(bf16[576,128]{1,0:T(8,128)(2,1)S(1)} %collective-permute-done.4.first), channel_id=1, source_target_pairs={{0,1},{1,0},{16,17},{17,16},{32,33},{33,32},{48,49},{49,48},{64,65... | collective-permute-start | bytes 442376 | tf_op jit(solution)/shard_map/ppermute | solution.py:49
  41.8 4.3 %collective-permute-start.9 = (bf16[2016,128]{1,0:T(8,128)(2,1)S(1)}, bf16[2016,128]{1,0:T(8,128)(2,1)S(1)}, u32[]{:S(2)}, u32[]{:S(2)}) collective-permute-start(bf16[2016,128]{1,0:T(8,128)(2,1)S(1)} %pad_maximum_fusion.bb), channel_id=1, source_target_pairs={{0,1},{1,0},{16,17},{17,16},{32,33},{33,32},{48,49},{49,48},{64,65... | collective-permute-start | bytes 1548296 | tf_op jit(solution)/shard_map/ppermute | solution.py:49
  43.4 2.6 %collective-permute-start.12 = (bf16[2016,128]{1,0:T(8,128)(2,1)S(1)}, bf16[2016,128]{1,0:T(8,128)(2,1)S(1)}, u32[]{:S(2)}, u32[]{:S(2)}) collective-permute-start(bf16[2016,128]{1,0:T(8,128)(2,1)S(1)} %collective-permute-done.8.dd), channel_id=1, source_target_pairs={{0,1},{1,0},{16,17},{17,16},{32,33},{33,32},{48,49},{49,48},{64,65... | collective-permute-start | bytes 1548296 | tf_op jit(solution)/shard_map/ppermute | solution.py:49
  44.5 3.1 %collective-permute-start.11 = (bf16[2016,128]{1,0:T(8,128)(2,1)S(1)}, bf16[2016,128]{1,0:T(8,128)(2,1)S(1)}, u32[]{:S(2)}, u32[]{:S(2)}) collective-permute-start(bf16[2016,128]{1,0:T(8,128)(2,1)S(1)} %collective-permute-done.7.xx), channel_id=1, source_target_pairs={{0,1},{1,0},{16,17},{17,16},{32,33},{33,32},{48,49},{49,48},{64,65... | collective-permute-start | bytes 1548296 | tf_op jit(solution)/shard_map/ppermute | solution.py:49
  46.0 2.3 %collective-permute-start.10 = (bf16[2016,128]{1,0:T(8,128)(2,1)S(1)}, bf16[2016,128]{1,0:T(8,128)(2,1)S(1)}, u32[]{:S(2)}, u32[]{:S(2)}) collective-permute-start(bf16[2016,128]{1,0:T(8,128)(2,1)S(1)} %collective-permute-done.5.yy), channel_id=1, source_target_pairs={{0,1},{1,0},{16,17},{17,16},{32,33},{33,32},{48,49},{49,48},{64,65... | collective-permute-start | bytes 1548296 | tf_op jit(solution)/shard_map/ppermute | solution.py:49
  64.9 1.6 %collective-permute-start.13 = (bf16[256,512]{1,0:T(8,128)(2,1)S(1)}, bf16[256,512]{1,0:T(8,128)(2,1)S(1)}, u32[]{:S(2)}, u32[]{:S(2)}) collective-permute-start(bf16[256,512]{1,0:T(8,128)(2,1)S(1)} %attend.1.own_ref), channel_id=1, source_target_pairs={{0,1},{1,0},{16,17},{17,16},{32,33},{33,32},{48,49},{49,48},{64,65... | collective-permute-start | bytes 786440 | tf_op jit(solution)/shard_map/ppermute | solution.py:49
  68.6 10.8 %collective-permute-start.15 = (bf16[448,256]{1,0:T(8,128)(2,1)S(1)}, bf16[448,256]{1,0:T(8,128)(2,1)S(1)}, u32[]{:S(2)}, u32[]{:S(2)}) collective-permute-start(bf16[448,256]{1,0:T(8,128)(2,1)S(1)} %get-tuple-element.35), channel_id=1, source_target_pairs={{0,12},{1,13},{16,28},{17,29},{32,44},{33,45},{48,60},{49,61},{64,... | collective-permute-start | bytes 688136 | tf_op jit(solution)/shard_map/ppermute | solution.py:49
  71.7 13.1 %collective-permute-start.16 = (bf16[448,256]{1,0:T(8,128)(2,1)S(1)}, bf16[448,256]{1,0:T(8,128)(2,1)S(1)}, u32[]{:S(2)}, u32[]{:S(2)}) collective-permute-start(bf16[448,256]{1,0:T(8,128)(2,1)S(1)} %get-tuple-element.36), channel_id=1, source_target_pairs={{0,10},{1,11},{16,26},{17,27},{32,42},{33,43},{48,58},{49,59},{64,... | collective-permute-start | bytes 688136 | tf_op jit(solution)/shard_map/ppermute | solution.py:49
  73.1 15.7 %collective-permute-start.17 = (bf16[448,256]{1,0:T(8,128)(2,1)S(1)}, bf16[448,256]{1,0:T(8,128)(2,1)S(1)}, u32[]{:S(2)}, u32[]{:S(2)}) collective-permute-start(bf16[448,256]{1,0:T(8,128)(2,1)S(1)} %get-tuple-element.37), channel_id=1, source_target_pairs={{0,14},{1,15},{16,30},{17,31},{32,46},{33,47},{48,62},{49,63},{64,... | collective-permute-start | bytes 688136 | tf_op jit(solution)/shard_map/ppermute | solution.py:49
  76.8 13.6 %collective-permute-start.18 = (bf16[448,256]{1,0:T(8,128)(2,1)S(1)}, bf16[448,256]{1,0:T(8,128)(2,1)S(1)}, u32[]{:S(2)}, u32[]{:S(2)}) collective-permute-start(bf16[448,256]{1,0:T(8,128)(2,1)S(1)} %get-tuple-element.38), channel_id=1, source_target_pairs={{0,4},{1,5},{16,20},{17,21},{32,36},{33,37},{48,52},{49,53},{64,68... | collective-permute-start | bytes 688136 | tf_op jit(solution)/shard_map/ppermute | solution.py:49
  76.9 16.5 %collective-permute-start.19 = (bf16[448,256]{1,0:T(8,128)(2,1)S(1)}, bf16[448,256]{1,0:T(8,128)(2,1)S(1)}, u32[]{:S(2)}, u32[]{:S(2)}) collective-permute-start(bf16[448,256]{1,0:T(8,128)(2,1)S(1)} %get-tuple-element.39), channel_id=1, source_target_pairs={{0,8},{1,9},{16,24},{17,25},{32,40},{33,41},{48,56},{49,57},{64,72... | collective-permute-start | bytes 688136 | tf_op jit(solution)/shard_map/ppermute | solution.py:49
  79.4 15.8 %collective-permute-start.20 = (bf16[448,256]{1,0:T(8,128)(2,1)S(1)}, bf16[448,256]{1,0:T(8,128)(2,1)S(1)}, u32[]{:S(2)}, u32[]{:S(2)}) collective-permute-start(bf16[448,256]{1,0:T(8,128)(2,1)S(1)} %get-tuple-element.40), channel_id=1, source_target_pairs={{0,2},{1,3},{16,18},{17,19},{32,34},{33,35},{48,50},{49,51},{64,66... | collective-permute-start | bytes 688136 | tf_op jit(solution)/shard_map/ppermute | solution.py:49
  84.8 10.5 %collective-permute-start.21 = (bf16[448,256]{1,0:T(8,128)(2,1)S(1)}, bf16[448,256]{1,0:T(8,128)(2,1)S(1)}, u32[]{:S(2)}, u32[]{:S(2)}) collective-permute-start(bf16[448,256]{1,0:T(8,128)(2,1)S(1)} %get-tuple-element.41), channel_id=1, source_target_pairs={{0,6},{1,7},{16,22},{17,23},{32,38},{33,39},{48,54},{49,55},{64,70... | collective-permute-start | bytes 688136 | tf_op jit(solution)/shard_map/ppermute | solution.py:49
  (7 other events, 41.8 us)

commit v3 on v2

--- a/solution.py
+++ b/solution.py
@@ -99,15 +99,22 @@
 ANY_SPEC = pl.BlockSpec(memory_space=pl.ANY)
 
 
-def pack_kernel(order_ref, cache_ref, table_ref, own_ref, slice_ref, part_ref, first_ref):
+def pack_kernel(order_ref, cache_any, table_any, own_ref, slice_ref, first_ref, cache_ref, table_ref, sems):
     xl, z, xh, y, c = me()
+    loads = (
+        pltpu.make_async_copy(table_any, table_ref, sems.at[0]),
+        pltpu.make_async_copy(cache_any, cache_ref, sems.at[1]),
+    )
+    for load in loads:
+        load.start()
+    for load in loads:
+        load.wait()
     for half in range(2):
         tokens = pl.ds(own_rows(order_ref, half), SPAN)
         cos, sin = cos_sin(table_ref, span_of(order_ref, xl, z, half))
         own_ref[half, 0:LAT, :] = cache_ref[0:LAT, tokens]
         own_ref[half, LAT:KEY, :] = rotated(cache_ref[LAT:KEY, tokens], cos, sin).astype(BF16)
     slice_ref[...] = own_ref[y % 2]
-    part_ref[...] = own_ref[y % 2, pl.ds(pl.multiple_of(c * (KEY // 2), 32), KEY // 2), :]
     first_ref[...] = own_ref[c]
 
 
@@ -117,12 +124,16 @@
         out_shape=(
             jax.ShapeDtypeStruct((2, KEY, SPAN), BF16),
             jax.ShapeDtypeStruct((KEY, SPAN), BF16),
-            jax.ShapeDtypeStruct((KEY // 2, SPAN), BF16),
             jax.ShapeDtypeStruct((KEY, SPAN), BF16),
         ),
-        in_specs=[SMEM_SPEC, VMEM_SPEC, VMEM_SPEC],
-        out_specs=(VMEM_SPEC,) * 4,
-        compiler_params=vmem(16),
+        in_specs=[SMEM_SPEC, ANY_SPEC, ANY_SPEC],
+        out_specs=(VMEM_SPEC,) * 3,
+        scratch_shapes=[
+            pltpu.VMEM((KEY, 2 * SPAN), BF16),
+            pltpu.VMEM((4, ROPE // 2, SPAN), F32),
+            pltpu.SemaphoreType.DMA((2,)),
+        ],
+        compiler_params=vmem(60),
         name="pack_keys",
     )(order, cache, table)
 
@@ -156,36 +167,36 @@
 STEPS = 7
 
 
-def attend_kernel(
-    order_ref, q_ref, va_ref, own, first, first2, bb, yy, xx, dd, bb2, yy2, xx2, dd2,
-    out_ref, keys, scores, peaks, total, acc, sems,
-):
+HALF = KEY // 2
+BUNDLE = 3 * KEY + HALF
+SIZES = (2 * KEY,) + (KEY,) + (BUNDLE,) * 4 + (KEY,) + (BUNDLE,) * 4
+BASES = tuple(sum(SIZES[:i]) for i in range(len(SIZES) + 1))
+
+
+def attend_kernel(order_ref, q_ref, va_ref, keys, out_ref, top_row, end_row, scores, peaks, total, acc):
     xl, z, xh, y, c = me()
     s = y % 2
     w = 1 - 2 * c
-    copies = []
-
-    def fetch(src, dst):
-        copy = pltpu.make_async_copy(src, dst, sems.at[len(copies)])
-        copy.start()
-        copies.append(copy)
+
+    def put(span, row, end=None):
+        top_row[span] = row
+        end_row[span] = row + HALF if end is None else end
 
     for half in range(2):
-        fetch(own.at[half], keys.at[span_of(order_ref, xl, z, half)])
-    fetch(first, keys.at[span_of(order_ref, 1 - xl, z, c)])
-    fetch(first2, keys.at[span_of(order_ref, 1 - xl, z, 1 - c)])
-    kinds = ((xl, s), (xl, 1 - s), (1 - xl, s), (1 - xl, 1 - s))
-    for (px, ph), mine, other in zip(kinds, (bb, yy, xx, dd), (bb2, yy2, xx2, dd2)):
+        put(span_of(order_ref, xl, z, half), BASES[0] + KEY * half)
+    put(span_of(order_ref, 1 - xl, z, c), BASES[1])
+    put(span_of(order_ref, 1 - xl, z, 1 - c), BASES[6])
+    for k, (px, ph) in enumerate(((xl, s), (xl, 1 - s), (1 - xl, s), (1 - xl, 1 - s))):
+        mine, other = BASES[2 + k], BASES[7 + k]
         for t in (1, 2, 3):
-            rows = pl.ds((t - 1) * KEY, KEY)
-            fetch(mine.at[rows], keys.at[span_of(order_ref, px, z - w * t, ph)])
-            fetch(other.at[rows], keys.at[span_of(order_ref, px, z + w * t, ph)])
-        far = span_of(order_ref, px, z + 4, ph)
-        rows = pl.ds(3 * KEY, KEY // 2)
-        fetch(mine.at[rows], keys.at[far, pl.ds(pl.multiple_of(KEY // 2 * c, 32), KEY // 2)])
-        fetch(other.at[rows], keys.at[far, pl.ds(pl.multiple_of(KEY // 2 * (1 - c), 32), KEY // 2)])
-    for copy in copies:
-        copy.wait()
+            put(span_of(order_ref, px, z - w * t, ph), mine + KEY * (t - 1))
+            put(span_of(order_ref, px, z + w * t, ph), other + KEY * (t - 1))
+        ends = (mine + 3 * KEY, other + 3 * KEY)
+        put(
+            span_of(order_ref, px, z + 4, ph),
+            jnp.where(c == 0, ends[0], ends[1]),
+            jnp.where(c == 0, ends[1], ends[0]),
+        )
 
     lower = span_of(order_ref, xl, z, 0)
     upper = 31 - lower
@@ -194,12 +205,16 @@
     wide = BLOCK * SPAN
 
     def tokens(block, rows):
-        return jnp.concatenate([keys[BLOCK * block + i, rows, :] for i in range(BLOCK)], axis=1)
+        columns = []
+        for i in range(BLOCK):
+            top = pl.multiple_of(top_row[BLOCK * block + i], 32)
+            end = pl.multiple_of(end_row[BLOCK * block + i], 32)
+            parts = [keys[pl.ds(top, HALF), :], keys[pl.ds(end, rows - HALF), :]]
+            columns.append(jnp.concatenate(parts, axis=0))
+        return jnp.concatenate(columns, axis=1)
 
     def score(half, block):
-        latent = jnp.dot(q_ref[half, :, 0:LAT], tokens(block, slice(0, LAT)), preferred_element_type=F32)
-        turned = jnp.dot(q_ref[half, :, LAT:KEY], tokens(block, slice(LAT, KEY)), preferred_element_type=F32)
-        return latent + turned
+        return jnp.dot(q_ref[half], tokens(block, KEY), preferred_element_type=F32)
 
     def widest(value):
         parts = [value[:, 128 * i : 128 * (i + 1)] for i in range(BLOCK)]
@@ -233,7 +248,7 @@
         parts = [jnp.exp2(scores[i, :, 128 * j : 128 * (j + 1)] * scale - top) for j in range(BLOCK)]
         weights = jnp.concatenate([part.astype(BF16) for part in parts], axis=1)
         product = lax.dot_general(
-            weights, tokens(block, slice(0, LAT)), (((1,), (1,)), ((), ())), preferred_element_type=F32
+            weights, tokens(block, LAT), (((1,), (1,)), ((), ())), preferred_element_type=F32
         )
         return (parts[0] + parts[1]) + (parts[2] + parts[3]), product
 
@@ -249,31 +264,31 @@
         rows = own_rows(order_ref, half)
         for h in range(HEADS):
             part = slice(h * SPAN, (h + 1) * SPAN)
-            bottom = jnp.sum(total[half, part, :], axis=1, keepdims=True)
-            context = (acc[half, part, :] / bottom).astype(BF16)
+            share = 1.0 / jnp.sum(total[half, part, :], axis=1, keepdims=True)
+            context = (acc[half, part, :] * share).astype(BF16)
             value = jnp.dot(context, va_ref[h], preferred_element_type=F32)
             out_ref[pl.ds(rows, SPAN), h * 128 : (h + 1) * 128] = value.astype(BF16)
 
 
-def attend(order, q, value_absorb, pieces):
+def attend(order, q, value_absorb, keys):
     rows = HEADS * SPAN
     return pl.pallas_call(
         attend_kernel,
         out_shape=jax.ShapeDtypeStruct((2 * SPAN, HEADS * 128), BF16),
-        in_specs=[SMEM_SPEC, VMEM_SPEC, VMEM_SPEC] + [ANY_SPEC] * len(pieces),
+        in_specs=[SMEM_SPEC] + [VMEM_SPEC] * 3,
         out_specs=VMEM_SPEC,
         scratch_shapes=[
-            pltpu.VMEM((32, KEY, SPAN), BF16),
+            pltpu.SMEM((32,), jnp.int32),
+            pltpu.SMEM((32,), jnp.int32),
             pltpu.VMEM((STEPS + 2, rows, BLOCK * SPAN), F32),
             pltpu.VMEM((STEPS + 2, rows, 128), F32),
             pltpu.VMEM((2, rows, 128), F32),
             pltpu.VMEM((2, rows, LAT), F32),
-            pltpu.SemaphoreType.DMA((40,)),
         ],
         compiler_params=vmem(40),
         cost_estimate=pl.CostEstimate(flops=6_000_000_000, bytes_accessed=8_000_000, transcendentals=2_200_000),
         name="attend",
-    )(order, q, value_absorb, *pieces)
+    )(order, q, value_absorb, keys)
 
 
 def columns_kernel(weight_ref, wait_ref, keep_ref, give_ref):
@@ -305,7 +320,7 @@
     )(weight, wait)
 
 
-OFFSETS = [(1, 2), (1, 1), (1, 3), (0, 2), (1, 0), (0, 1), (0, 3), (0, 0)]
+OFFSETS = [(1, 2), (1, 1), (1, 3), (1, 0), (0, 2), (0, 1), (0, 3), (0, 0)]
 
 
 def project_kernel(own_ref, other_ref, keep_ref, got_ref, *outs):
@@ -333,30 +348,38 @@
 
 def body(queries, latent_cache, key_absorb, value_absorb, out_weight, span_order):
     table = tables()
-    own, piece, part, first_half = pack(span_order, latent_cache.T, table)
-
+    own, piece, first_half = pack(span_order, latent_cache.T, table)
+
+    ways = (along(dy=1), along(dx=1), along(dx=1, dy=1))
+    c = lax.axis_index("head") % NC
+    b3 = send(piece, along(dz=3))
+    b4 = send(jnp.where(c == 0, piece[:HALF], piece[HALF:]), along(dz=4))
+    b2 = send(piece, along(dz=2))
     b1 = send(piece, along(dz=1))
-    b2 = send(piece, along(dz=2))
-    b3 = send(piece, along(dz=3))
-    b4 = send(part, along(dz=4))
     first = send(first_half, along(dx=1))
     keep, give = split_columns(out_weight, piece)
-    bb, give, first = lax.optimization_barrier((jnp.concatenate([b1, b2, b3, b4], axis=0), give, first))
-    yy, xx, dd = (send(bb, step) for step in (along(dy=1), along(dx=1), along(dx=1, dy=1)))
+    bundle, give, first = lax.optimization_barrier((jnp.concatenate([b1, b2, b3, b4], axis=0), give, first))
+    bundles = [send(bundle, step) for step in (along(dy=1), along(dx=1), along(dx=1, dy=1))]
     got = send(give, swap)
-    bb2 = send(bb, swap)
-    first2 = send(first, swap)
+    early = jnp.concatenate([first, bundle], axis=0)
+    early2 = send(early, swap)
+    early2, queries = lax.optimization_barrier((early2, queries))
     q = absorb(span_order, queries.transpose(1, 2, 0), key_absorb, table)
-    yy, q = lax.optimization_barrier((yy, q))
-    yy2, xx2, dd2 = (send(value, swap) for value in (yy, xx, dd))
-
-    values = attend(span_order, q, value_absorb, (own, first, first2, bb, yy, xx, dd, bb2, yy2, xx2, dd2))
-    other = send(values, swap)
-    terms = project(values, other, keep, got)
-    landed = [
-        term if (dx, dy) == (0, 0) else send(term, lambda x, y, z, c, dx=dx, dy=dy: (x + 2 * dx, y + dy, z, c))
-        for term, (dx, dy) in zip(terms, OFFSETS)
-    ]
+    bundles[1], q = lax.optimization_barrier((bundles[1], q))
+    bundles2 = [send(value, swap) for value in bundles]
+    keys = jnp.concatenate([own.reshape(2 * KEY, SPAN), early] + bundles + [early2] + bundles2, axis=0)
+
+    values = attend(span_order, q, value_absorb, keys)
+    terms = project(values, send(values, swap), keep, got)
+
+    def deliver(term, dx, dy):
+        return send(term, lambda x, y, z, c: (x + 2 * dx, y + dy, z, c))
+
+    landed = [deliver(term, *offset) for term, offset in zip(terms[:5], OFFSETS)]
+    rest = lax.optimization_barrier((landed[0], *terms[5:7]))
+    landed[0] = rest[0]
+    landed += [deliver(term, *offset) for term, offset in zip(rest[1:], OFFSETS[5:])]
+    landed.append(terms[7])
     return functools.reduce(jnp.add, [term.astype(F32) for term in landed]).astype(BF16).T
 
 

time: 96.4 us -> 88.4 us (0.917)
  Pallas kernels: 24 us -> 18.9 us
  starting transfers between devices: 37.7 us -> 35.9 us
  waiting for transfers between devices: 27.8 us -> 26.4 us
  other arithmetic: 0.96 us -> 1.97 us
    pallas_call x1, Pallas kernels: 16.6 us -> 9.62 us  [attend(): pl.pallas_call(attend_kernel, out_shape=jax.ShapeDtypeStruct((2 * SPAN, H...]
    pallas_call x1, Pallas kernels: 0.72 us -> 2.58 us  [pack(): pl.pallas_call(pack_kernel, out_shape=(jax.ShapeDtypeStruct((2, KEY, SPAN...]
    ppermute x22 -> x21, starting transfers between devices: 37.7 us -> 35.9 us  [send(): return lax.ppermute(value, AXES, routes(step))]
    ppermute x22 -> x21, waiting for transfers between devices: 27.8 us -> 26.4 us  [send(): return lax.ppermute(value, AXES, routes(step))]
    unnamed x18 -> x25, local copies, waits for them, and re-layouts: 5.56 us -> 4.56 us
    select_n x0 -> x1, other arithmetic: none -> 0.97 us  [body(): b4 = send(jnp.where(c == 0, piece[:HALF], piece[HALF:]), along(dz=4))]
  transfers between devices with their start and end apart: 22 -> 21, of which waited for: 11 -> 8; matrix products, arithmetic and copies ran while one was open for 0% -> 2% of each run, Pallas kernels for 22% -> 16%
where the time goes in v3:
time: 88.4 us; the launch traced here: 88.2 us
  starting transfers between devices  35.9 us (41%)
  waiting for transfers between devices  26.4 us (30%)
  Pallas kernels  18.9 us (21%)
  local copies, waits for them, and re-layouts  4.63 us (5%)
  other arithmetic  1.97 us (2%)
    ppermute x21, starting transfers between devices, send(): return lax.ppermute(value, AXES, routes(step))  35.9 us
    ppermute x21, waiting for transfers between devices, send(): return lax.ppermute(value, AXES, routes(step))  26.4 us
    pallas_call x1, Pallas kernels, attend(): pl.pallas_call(attend_kernel, out_shape=jax.ShapeDtypeStruct((2 * SPAN, H...  9.62 us
    unnamed x25, local copies, waits for them, and re-layouts  4.56 us
    pallas_call x1, Pallas kernels, split_columns(): pl.pallas_call(columns_kernel, grid=(8,), out_shape=(jax.ShapeDtypeStruct...  3.6 us
    pallas_call x1, Pallas kernels, pack(): pl.pallas_call(pack_kernel, out_shape=(jax.ShapeDtypeStruct((2, KEY, SPAN...  2.58 us
    pallas_call x1, Pallas kernels, project(): pl.pallas_call(project_kernel, out_shape=(jax.ShapeDtypeStruct((448, 256)...  2.08 us
  transfers between devices with their start and end apart: 21, of which 8 were waited for; matrix products, arithmetic and copies ran while one was open for 2% of the time, Pallas kernels for 16%

profile of v3, /device:TPU:1, one launch (start us, length us, event | category | flops | bytes accessed | tf_op | source)
XLA Modules:
  0.0 88.2 jit_solution(4821495935051582836)
XLA Ops:
  0.0 2.6 %pack_keys.1 = (bf16[2,576,128]{2,1,0:T(8,128)(2,1)}, bf16[576,128]{1,0:T(8,128)(2,1)}, bf16[576,128]{1,0:T(8,128)(2,1)}) custom-call(s32[32]{0:T(128)} %order_ref.5, bf16[576,256]{1,0:T(8,128)(2,1)} %bitcast.6, f32[4,32,128]{2,1,0:T(8,128)} %constant.20.clone.table_any.table_ref), custom_call_target="tpu_custom_call" | custom-call | tf_op jit(solution)/shard_map/pack_keys/pallas_call | solution.py:122
  2.6 6.5 %collective-permute-start = (bf16[576,128]{1,0:T(8,128)(2,1)}, bf16[576,128]{1,0:T(8,128)(2,1)S(1)}, u32[]{:S(2)}, u32[]{:S(2)}) collective-permute-start(bf16[576,128]{1,0:T(8,128)(2,1)} %get-tuple-element.28.wait_ref), channel_id=1, source_target_pairs={{0,16},{1,113},{16,32},{17,1},{32,48},{33,17},{48,64},{49,33},{64,... | collective-permute-start | bytes 442376 | tf_op jit(solution)/shard_map/ppermute | solution.py:49
  11.7 4.6 %collective-permute-start.3 = (bf16[288,128]{1,0:T(8,128)(2,1)S(1)}, bf16[288,128]{1,0:T(8,128)(2,1)S(1)}, u32[]{:S(2)}, u32[]{:S(2)}) collective-permute-start(bf16[288,128]{1,0:T(8,128)(2,1)S(1)} %slice_select_fusion), channel_id=1, source_target_pairs={{0,64},{1,65},{16,80},{17,81},{32,96},{33,97},{48,112},{49,113},{6... | collective-permute-start | bytes 221192 | tf_op jit(solution)/shard_map/ppermute | solution.py:49
  16.2 2.5 %collective-permute-start.4 = (bf16[576,128]{1,0:T(8,128)(2,1)}, bf16[576,128]{1,0:T(8,128)(2,1)S(1)}, u32[]{:S(2)}, u32[]{:S(2)}) collective-permute-start(bf16[576,128]{1,0:T(8,128)(2,1)} %get-tuple-element.30), channel_id=1, source_target_pairs={{0,128},{1,137},{16,144},{17,153},{32,160},{33,169},{48,176},{49,1... | collective-permute-start | bytes 442376 | tf_op jit(solution)/shard_map/ppermute | solution.py:49
  18.7 3.1 %copy-done = bf16[512,7168]{1,0:T(8,128)(2,1)S(1)} copy-done((bf16[512,7168]{1,0:T(8,128)(2,1)S(1)}, bf16[512,7168]{1,0:T(8,128)(2,1)}, u32[]{:S(2)}) %copy-start) | copy-done | bytes 7340056
  22.7 3.6 %split_columns.1 = (bf16[3584,512]{1,0:T(8,128)(2,1)S(1)}, bf16[3584,512]{1,0:T(8,128)(2,1)S(1)}) custom-call(bf16[512,7168]{1,0:T(8,128)(2,1)S(1)} %copy-done, bf16[576,128]{1,0:T(8,128)(2,1)S(1)} %copy-done.1), custom_call_target="tpu_custom_call" | custom-call | bytes 15000000 | tf_op jit(solution)/shard_map/split_columns/pallas_call | solution.py:311
  26.5 2.8 %collective-permute-start.7 = (bf16[2016,128]{1,0:T(8,128)(2,1)S(1)}, bf16[2016,128]{1,0:T(8,128)(2,1)S(1)}, u32[]{:S(2)}, u32[]{:S(2)}) collective-permute-start(bf16[2016,128]{1,0:T(8,128)(2,1)S(1)} %pad_maximum_fusion.1), channel_id=1, source_target_pairs={{0,2},{1,7},{16,18},{17,23},{32,34},{33,39},{48,50},{49,55},{64,66... | collective-permute-start | bytes 1548296 | tf_op jit(solution)/shard_map/ppermute | solution.py:49
  29.3 1.7 %collective-permute-start.8 = (bf16[2016,128]{1,0:T(8,128)(2,1)S(1)}, bf16[2016,128]{1,0:T(8,128)(2,1)S(1)}, u32[]{:S(2)}, u32[]{:S(2)}) collective-permute-start(bf16[2016,128]{1,0:T(8,128)(2,1)S(1)} %pad_maximum_fusion.1), channel_id=1, source_target_pairs={{0,130},{1,143},{16,146},{17,159},{32,162},{33,175},{48,178},{49,1... | collective-permute-start | bytes 1548296 | tf_op jit(solution)/shard_map/ppermute | solution.py:49
  31.3 1.5 %collective-permute-start.5 = (bf16[2016,128]{1,0:T(8,128)(2,1)S(1)}, bf16[2016,128]{1,0:T(8,128)(2,1)S(1)}, u32[]{:S(2)}, u32[]{:S(2)}) collective-permute-start(bf16[2016,128]{1,0:T(8,128)(2,1)S(1)} %pad_maximum_fusion.1), channel_id=1, source_target_pairs={{0,128},{1,137},{16,144},{17,153},{32,160},{33,169},{48,176},{49,1... | collective-permute-start | bytes 1548296 | tf_op jit(solution)/shard_map/ppermute | solution.py:49
  32.9 8.0 %collective-permute-done.7 = bf16[2016,128]{1,0:T(8,128)(2,1)S(1)} collective-permute-done((bf16[2016,128]{1,0:T(8,128)(2,1)S(1)}, bf16[2016,128]{1,0:T(8,128)(2,1)S(1)}, u32[]{:S(2)}, u32[]{:S(2)}) %collective-permute-start.7) | collective-permute-done | bytes 516128 | tf_op jit(solution)/shard_map/ppermute | solution.py:49
  40.9 2.0 %collective-permute-start.9 = (bf16[2016,128]{1,0:T(8,128)(2,1)S(1)}, bf16[2016,128]{1,0:T(8,128)(2,1)S(1)}, u32[]{:S(2)}, u32[]{:S(2)}) collective-permute-start(bf16[2016,128]{1,0:T(8,128)(2,1)S(1)} %collective-permute-done.7), channel_id=1, source_target_pairs={{0,1},{1,0},{16,17},{17,16},{32,33},{33,32},{48,49},{49,48},{64,65... | collective-permute-start | bytes 1548296 | tf_op jit(solution)/shard_map/ppermute | solution.py:49
  44.0 1.5 %collective-permute-start.10 = (bf16[2016,128]{1,0:T(8,128)(2,1)S(1)}, bf16[2016,128]{1,0:T(8,128)(2,1)S(1)}, u32[]{:S(2)}, u32[]{:S(2)}) collective-permute-start(bf16[2016,128]{1,0:T(8,128)(2,1)S(1)} %collective-permute-done.5), channel_id=1, source_target_pairs={{0,1},{1,0},{16,17},{17,16},{32,33},{33,32},{48,49},{49,48},{64,65... | collective-permute-start | bytes 1548296 | tf_op jit(solution)/shard_map/ppermute | solution.py:49
  45.8 1.2 %collective-permute-done.10 = bf16[2016,128]{1,0:T(8,128)(2,1)S(1)} collective-permute-done((bf16[2016,128]{1,0:T(8,128)(2,1)S(1)}, bf16[2016,128]{1,0:T(8,128)(2,1)S(1)}, u32[]{:S(2)}, u32[]{:S(2)}) %collective-permute-start.10) | collective-permute-done | bytes 516128 | tf_op jit(solution)/shard_map/ppermute | solution.py:49
  47.2 9.6 %attend.1.own_ref = bf16[256,512]{1,0:T(8,128)(2,1)S(1)} custom-call(s32[32]{0:T(128)S(1)} %copy-done.5, bf16[2,512,576]{2,1,0:T(8,128)(2,1)S(1)} %absorb_queries.1.q_ref, bf16[4,512,128]{2,1,0:T(8,128)(2,1)S(1)} %copy-done.6, bf16[18432,128]{1,0:T(8,128)(2,1)S(1)} %constant_dynamic-update-slice_fusion.keys), custom_call_target="tpu_custom_call" | custom-call | flops 6000000000 | bytes 8000000 | tf_op jit(solution)/shard_map/attend/pallas_call | solution.py:275
  58.4 2.1 %project.1 = (bf16[448,256]{1,0:T(8,128)(2,1)S(1)}, bf16[448,256]{1,0:T(8,128)(2,1)S(1)}, bf16[448,256]{1,0:T(8,128)(2,1)S(1)}, bf16[448,256]{1,0:T(8,128)(2,1)S...) custom-call(bf16[256,512]{1,0:T(8,128)(2,1)S(1)} %attend.1.own_ref, ...), custom_call_target="tpu_custom_call" | custom-call | flops 1900000000 | bytes 8000000 | tf_op jit(solution)/shard_map/project/pallas_call | solution.py:338
  60.5 2.3 %collective-permute-start.14 = (bf16[448,256]{1,0:T(8,128)(2,1)S(1)}, bf16[448,256]{1,0:T(8,128)(2,1)S(1)}, u32[]{:S(2)}, u32[]{:S(2)}) collective-permute-start(bf16[448,256]{1,0:T(8,128)(2,1)S(1)} %get-tuple-element.40), channel_id=1, source_target_pairs={{0,12},{1,13},{16,28},{17,29},{32,44},{33,45},{48,60},{49,61},{64,... | collective-permute-start | bytes 688136 | tf_op jit(solution)/shard_map/ppermute | solution.py:49
  62.9 2.1 %collective-permute-start.15 = (bf16[448,256]{1,0:T(8,128)(2,1)S(1)}, bf16[448,256]{1,0:T(8,128)(2,1)S(1)}, u32[]{:S(2)}, u32[]{:S(2)}) collective-permute-start(bf16[448,256]{1,0:T(8,128)(2,1)S(1)} %get-tuple-element.44), channel_id=1, source_target_pairs={{0,10},{1,11},{16,26},{17,27},{32,42},{33,43},{48,58},{49,59},{64,... | collective-permute-start | bytes 688136 | tf_op jit(solution)/shard_map/ppermute | solution.py:49
  65.0 3.0 %collective-permute-start.16 = (bf16[448,256]{1,0:T(8,128)(2,1)S(1)}, bf16[448,256]{1,0:T(8,128)(2,1)S(1)}, u32[]{:S(2)}, u32[]{:S(2)}) collective-permute-start(bf16[448,256]{1,0:T(8,128)(2,1)S(1)} %get-tuple-element.45), channel_id=1, source_target_pairs={{0,14},{1,15},{16,30},{17,31},{32,46},{33,47},{48,62},{49,63},{64,... | collective-permute-start | bytes 688136 | tf_op jit(solution)/shard_map/ppermute | solution.py:49
  68.0 1.7 %collective-permute-start.17 = (bf16[448,256]{1,0:T(8,128)(2,1)S(1)}, bf16[448,256]{1,0:T(8,128)(2,1)S(1)}, u32[]{:S(2)}, u32[]{:S(2)}) collective-permute-start(bf16[448,256]{1,0:T(8,128)(2,1)S(1)} %get-tuple-element.46), channel_id=1, source_target_pairs={{0,8},{1,9},{16,24},{17,25},{32,40},{33,41},{48,56},{49,57},{64,72... | collective-permute-start | bytes 688136 | tf_op jit(solution)/shard_map/ppermute | solution.py:49
  70.1 1.2 %collective-permute-done.14 = bf16[448,256]{1,0:T(8,128)(2,1)S(1)} collective-permute-done((bf16[448,256]{1,0:T(8,128)(2,1)S(1)}, bf16[448,256]{1,0:T(8,128)(2,1)S(1)}, u32[]{:S(2)}, u32[]{:S(2)}) %collective-permute-start.14) | collective-permute-done | bytes 229408 | tf_op jit(solution)/shard_map/ppermute | solution.py:49
  72.3 4.4 %collective-permute-done.15 = bf16[448,256]{1,0:T(8,128)(2,1)S(1)} collective-permute-done((bf16[448,256]{1,0:T(8,128)(2,1)S(1)}, bf16[448,256]{1,0:T(8,128)(2,1)S(1)}, u32[]{:S(2)}, u32[]{:S(2)}) %collective-permute-start.15) | collective-permute-done | bytes 229408 | tf_op jit(solution)/shard_map/ppermute | solution.py:49
  76.7 3.9 %collective-permute-done.16 = bf16[448,256]{1,0:T(8,128)(2,1)S(1)} collective-permute-done((bf16[448,256]{1,0:T(8,128)(2,1)S(1)}, bf16[448,256]{1,0:T(8,128)(2,1)S(1)}, u32[]{:S(2)}, u32[]{:S(2)}) %collective-permute-start.16) | collective-permute-done | bytes 229408 | tf_op jit(solution)/shard_map/ppermute | solution.py:49
  80.6 4.9 %collective-permute-done.17 = bf16[448,256]{1,0:T(8,128)(2,1)S(1)} collective-permute-done((bf16[448,256]{1,0:T(8,128)(2,1)S(1)}, bf16[448,256]{1,0:T(8,128)(2,1)S(1)}, u32[]{:S(2)}, u32[]{:S(2)}) %collective-permute-start.17) | collective-permute-done | bytes 229408 | tf_op jit(solution)/shard_map/ppermute | solution.py:49
  85.6 1.7 %collective-permute-done.19 = bf16[448,256]{1,0:T(8,128)(2,1)S(1)} collective-permute-done((bf16[448,256]{1,0:T(8,128)(2,1)S(1)}, bf16[448,256]{1,0:T(8,128)(2,1)S(1)}, u32[]{:S(2)}, u32[]{:S(2)}) %collective-permute-start.19) | collective-permute-done | bytes 229408 | tf_op jit(solution)/shard_map/ppermute | solution.py:49
  (53 shorter events, 9.5 us)
Async XLA Ops:
  2.6 23.8 %collective-permute-start = (bf16[576,128]{1,0:T(8,128)(2,1)}, bf16[576,128]{1,0:T(8,128)(2,1)S(1)}, u32[]{:S(2)}, u32[]{:S(2)}) collective-permute-start(bf16[576,128]{1,0:T(8,128)(2,1)} %get-tuple-element.28.wait_ref), channel_id=1, source_target_pairs={{0,16},{1,113},{16,32},{17,1},{32,48},{33,17},{48,64},{49,33},{64,... | collective-permute-start | bytes 442376 | tf_op jit(solution)/shard_map/ppermute | solution.py:49
  9.1 17.3 %collective-permute-start.1 = (bf16[576,128]{1,0:T(8,128)(2,1)}, bf16[576,128]{1,0:T(8,128)(2,1)S(1)}, u32[]{:S(2)}, u32[]{:S(2)}) collective-permute-start(bf16[576,128]{1,0:T(8,128)(2,1)} %get-tuple-element.28.wait_ref), channel_id=1, source_target_pairs={{0,32},{1,97},{16,48},{17,113},{32,64},{33,1},{48,80},{49,17},{64,... | collective-permute-start | bytes 442376 | tf_op jit(solution)/shard_map/ppermute | solution.py:49
  10.2 16.1 %collective-permute-start.2 = (bf16[576,128]{1,0:T(8,128)(2,1)}, bf16[576,128]{1,0:T(8,128)(2,1)S(1)}, u32[]{:S(2)}, u32[]{:S(2)}) collective-permute-start(bf16[576,128]{1,0:T(8,128)(2,1)} %get-tuple-element.28.wait_ref), channel_id=1, source_target_pairs={{0,48},{1,81},{16,64},{17,97},{32,80},{33,113},{48,96},{49,1},{64,... | collective-permute-start | bytes 442376 | tf_op jit(solution)/shard_map/ppermute | solution.py:49
  11.7 14.7 %collective-permute-start.3 = (bf16[288,128]{1,0:T(8,128)(2,1)S(1)}, bf16[288,128]{1,0:T(8,128)(2,1)S(1)}, u32[]{:S(2)}, u32[]{:S(2)}) collective-permute-start(bf16[288,128]{1,0:T(8,128)(2,1)S(1)} %slice_select_fusion), channel_id=1, source_target_pairs={{0,64},{1,65},{16,80},{17,81},{32,96},{33,97},{48,112},{49,113},{6... | collective-permute-start | bytes 221192 | tf_op jit(solution)/shard_map/ppermute | solution.py:49
  16.2 10.2 %collective-permute-start.4 = (bf16[576,128]{1,0:T(8,128)(2,1)}, bf16[576,128]{1,0:T(8,128)(2,1)S(1)}, u32[]{:S(2)}, u32[]{:S(2)}) collective-permute-start(bf16[576,128]{1,0:T(8,128)(2,1)} %get-tuple-element.30), channel_id=1, source_target_pairs={{0,128},{1,137},{16,144},{17,153},{32,160},{33,169},{48,176},{49,1... | collective-permute-start | bytes 442376 | tf_op jit(solution)/shard_map/ppermute | solution.py:49
  22.7 20.3 %copy-start.3 = (bf16[256,4,192]{0,2,1:T(8,128)(2,1)S(1)}, bf16[256,4,192]{0,2,1:T(8,128)(2,1)}, u32[]{:S(2)}) copy-start(bf16[256,4,192]{0,2,1:T(8,128)(2,1)} %param.7) | copy-start | bytes 1179652
  22.7 20.3 %copy-start.4 = (f32[4,32,128]{2,1,0:T(8,128)S(1)}, f32[4,32,128]{2,1,0:T(8,128)}, u32[]{:S(2)}) copy-start(f32[4,32,128]{2,1,0:T(8,128)} %constant.20.clone.table_any.table_ref) | copy-start | bytes 196612
  22.7 20.3 %copy-start.5 = (s32[32]{0:T(128)S(1)}, s32[32]{0:T(128)}, u32[]{:S(2)}) copy-start(s32[32]{0:T(128)} %order_ref.5) | copy-start | bytes 388
  26.4 32.0 %collective-permute-start.13 = (bf16[3584,512]{1,0:T(8,128)(2,1)S(1)}, bf16[3584,512]{1,0:T(8,128)(2,1)S(1)}, u32[]{:S(2)}, u32[]{:S(2)}) collective-permute-start(bf16[3584,512]{1,0:T(8,128)(2,1)S(1)} %get-tuple-element.39), channel_id=1, source_target_pairs={{0,1},{1,0},{16,17},{17,16},{32,33},{33,32},{48,49},{49,48},{64,65... | collective-permute-start | bytes 11010056 | tf_op jit(solution)/shard_map/ppermute | solution.py:49
  26.5 14.4 %collective-permute-start.7 = (bf16[2016,128]{1,0:T(8,128)(2,1)S(1)}, bf16[2016,128]{1,0:T(8,128)(2,1)S(1)}, u32[]{:S(2)}, u32[]{:S(2)}) collective-permute-start(bf16[2016,128]{1,0:T(8,128)(2,1)S(1)} %pad_maximum_fusion.1), channel_id=1, source_target_pairs={{0,2},{1,7},{16,18},{17,23},{32,34},{33,39},{48,50},{49,55},{64,66... | collective-permute-start | bytes 1548296 | tf_op jit(solution)/shard_map/ppermute | solution.py:49
  29.3 13.5 %collective-permute-start.8 = (bf16[2016,128]{1,0:T(8,128)(2,1)S(1)}, bf16[2016,128]{1,0:T(8,128)(2,1)S(1)}, u32[]{:S(2)}, u32[]{:S(2)}) collective-permute-start(bf16[2016,128]{1,0:T(8,128)(2,1)S(1)} %pad_maximum_fusion.1), channel_id=1, source_target_pairs={{0,130},{1,143},{16,146},{17,159},{32,162},{33,175},{48,178},{49,1... | collective-permute-start | bytes 1548296 | tf_op jit(solution)/shard_map/ppermute | solution.py:49
  31.1 11.8 %collective-permute-start.6 = (bf16[2592,128]{1,0:T(8,128)(2,1)S(1)}, bf16[2592,128]{1,0:T(8,128)(2,1)S(1)}, u32[]{:S(2)}, u32[]{:S(2)}) collective-permute-start(bf16[2592,128]{1,0:T(8,128)(2,1)S(1)} %pad_maximum_fusion), channel_id=1, source_target_pairs={{0,1},{1,0},{16,17},{17,16},{32,33},{33,32},{48,49},{49,48},{64,65... | collective-permute-start | bytes 1990664 | tf_op jit(solution)/shard_map/ppermute | solution.py:49
  31.3 12.7 %collective-permute-start.5 = (bf16[2016,128]{1,0:T(8,128)(2,1)S(1)}, bf16[2016,128]{1,0:T(8,128)(2,1)S(1)}, u32[]{:S(2)}, u32[]{:S(2)}) collective-permute-start(bf16[2016,128]{1,0:T(8,128)(2,1)S(1)} %pad_maximum_fusion.1), channel_id=1, source_target_pairs={{0,128},{1,137},{16,144},{17,153},{32,160},{33,169},{48,176},{49,1... | collective-permute-start | bytes 1548296 | tf_op jit(solution)/shard_map/ppermute | solution.py:49
  40.9 4.8 %collective-permute-start.9 = (bf16[2016,128]{1,0:T(8,128)(2,1)S(1)}, bf16[2016,128]{1,0:T(8,128)(2,1)S(1)}, u32[]{:S(2)}, u32[]{:S(2)}) collective-permute-start(bf16[2016,128]{1,0:T(8,128)(2,1)S(1)} %collective-permute-done.7), channel_id=1, source_target_pairs={{0,1},{1,0},{16,17},{17,16},{32,33},{33,32},{48,49},{49,48},{64,65... | collective-permute-start | bytes 1548296 | tf_op jit(solution)/shard_map/ppermute | solution.py:49
  42.9 4.2 %collective-permute-start.11 = (bf16[2016,128]{1,0:T(8,128)(2,1)S(1)}, bf16[2016,128]{1,0:T(8,128)(2,1)S(1)}, u32[]{:S(2)}, u32[]{:S(2)}) collective-permute-start(bf16[2016,128]{1,0:T(8,128)(2,1)S(1)} %collective-permute-done.8), channel_id=1, source_target_pairs={{0,1},{1,0},{16,17},{17,16},{32,33},{33,32},{48,49},{49,48},{64,65... | collective-permute-start | bytes 1548296 | tf_op jit(solution)/shard_map/ppermute | solution.py:49
  44.0 3.0 %collective-permute-start.10 = (bf16[2016,128]{1,0:T(8,128)(2,1)S(1)}, bf16[2016,128]{1,0:T(8,128)(2,1)S(1)}, u32[]{:S(2)}, u32[]{:S(2)}) collective-permute-start(bf16[2016,128]{1,0:T(8,128)(2,1)S(1)} %collective-permute-done.5), channel_id=1, source_target_pairs={{0,1},{1,0},{16,17},{17,16},{32,33},{33,32},{48,49},{49,48},{64,65... | collective-permute-start | bytes 1548296 | tf_op jit(solution)/shard_map/ppermute | solution.py:49
  56.8 1.6 %collective-permute-start.12 = (bf16[256,512]{1,0:T(8,128)(2,1)S(1)}, bf16[256,512]{1,0:T(8,128)(2,1)S(1)}, u32[]{:S(2)}, u32[]{:S(2)}) collective-permute-start(bf16[256,512]{1,0:T(8,128)(2,1)S(1)} %attend.1.own_ref), channel_id=1, source_target_pairs={{0,1},{1,0},{16,17},{17,16},{32,33},{33,32},{48,49},{49,48},{64,65... | collective-permute-start | bytes 786440 | tf_op jit(solution)/shard_map/ppermute | solution.py:49
  60.5 10.8 %collective-permute-start.14 = (bf16[448,256]{1,0:T(8,128)(2,1)S(1)}, bf16[448,256]{1,0:T(8,128)(2,1)S(1)}, u32[]{:S(2)}, u32[]{:S(2)}) collective-permute-start(bf16[448,256]{1,0:T(8,128)(2,1)S(1)} %get-tuple-element.40), channel_id=1, source_target_pairs={{0,12},{1,13},{16,28},{17,29},{32,44},{33,45},{48,60},{49,61},{64,... | collective-permute-start | bytes 688136 | tf_op jit(solution)/shard_map/ppermute | solution.py:49
  62.9 13.8 %collective-permute-start.15 = (bf16[448,256]{1,0:T(8,128)(2,1)S(1)}, bf16[448,256]{1,0:T(8,128)(2,1)S(1)}, u32[]{:S(2)}, u32[]{:S(2)}) collective-permute-start(bf16[448,256]{1,0:T(8,128)(2,1)S(1)} %get-tuple-element.44), channel_id=1, source_target_pairs={{0,10},{1,11},{16,26},{17,27},{32,42},{33,43},{48,58},{49,59},{64,... | collective-permute-start | bytes 688136 | tf_op jit(solution)/shard_map/ppermute | solution.py:49
  65.0 15.6 %collective-permute-start.16 = (bf16[448,256]{1,0:T(8,128)(2,1)S(1)}, bf16[448,256]{1,0:T(8,128)(2,1)S(1)}, u32[]{:S(2)}, u32[]{:S(2)}) collective-permute-start(bf16[448,256]{1,0:T(8,128)(2,1)S(1)} %get-tuple-element.45), channel_id=1, source_target_pairs={{0,14},{1,15},{16,30},{17,31},{32,46},{33,47},{48,62},{49,63},{64,... | collective-permute-start | bytes 688136 | tf_op jit(solution)/shard_map/ppermute | solution.py:49
  68.0 17.6 %collective-permute-start.17 = (bf16[448,256]{1,0:T(8,128)(2,1)S(1)}, bf16[448,256]{1,0:T(8,128)(2,1)S(1)}, u32[]{:S(2)}, u32[]{:S(2)}) collective-permute-start(bf16[448,256]{1,0:T(8,128)(2,1)S(1)} %get-tuple-element.46), channel_id=1, source_target_pairs={{0,8},{1,9},{16,24},{17,25},{32,40},{33,41},{48,56},{49,57},{64,72... | collective-permute-start | bytes 688136 | tf_op jit(solution)/shard_map/ppermute | solution.py:49
  69.7 15.9 %collective-permute-start.18 = (bf16[448,256]{1,0:T(8,128)(2,1)S(1)}, bf16[448,256]{1,0:T(8,128)(2,1)S(1)}, u32[]{:S(2)}, u32[]{:S(2)}) collective-permute-start(bf16[448,256]{1,0:T(8,128)(2,1)S(1)} %get-tuple-element.47), channel_id=1, source_target_pairs={{0,4},{1,5},{16,20},{17,21},{32,36},{33,37},{48,52},{49,53},{64,68... | collective-permute-start | bytes 688136 | tf_op jit(solution)/shard_map/ppermute | solution.py:49
  71.3 15.9 %collective-permute-start.19 = (bf16[448,256]{1,0:T(8,128)(2,1)S(1)}, bf16[448,256]{1,0:T(8,128)(2,1)S(1)}, u32[]{:S(2)}, u32[]{:S(2)}) collective-permute-start(bf16[448,256]{1,0:T(8,128)(2,1)S(1)} %get-tuple-element.48), channel_id=1, source_target_pairs={{0,2},{1,3},{16,18},{17,19},{32,34},{33,35},{48,50},{49,51},{64,66... | collective-permute-start | bytes 688136 | tf_op jit(solution)/shard_map/ppermute | solution.py:49
  76.7 10.5 %collective-permute-start.20 = (bf16[448,256]{1,0:T(8,128)(2,1)S(1)}, bf16[448,256]{1,0:T(8,128)(2,1)S(1)}, u32[]{:S(2)}, u32[]{:S(2)}) collective-permute-start(bf16[448,256]{1,0:T(8,128)(2,1)S(1)} %get-tuple-element.49), channel_id=1, source_target_pairs={{0,6},{1,7},{16,22},{17,23},{32,38},{33,39},{48,54},{49,55},{64,70... | collective-permute-start | bytes 688136 | tf_op jit(solution)/shard_map/ppermute | solution.py:49
  (5 other events, 47.0 us)
